TPU v7x, 32 devices: a whole 2x2x4 slice. The times are simulated.
32 devices in a mesh: seq: 4 (over z), stream: 8 (over y, x, core).
Axes of the slice: x: 2, y: 2, z: 4, core: 2. Of those that a mesh axis runs over, the one named last changes fastest.
Arguments:
- frames: bfloat16 [16, 2048, 80], P('stream', 'seq'), may hold values from -6 to 6
- targets: int32 [16, 2048], P('stream', 'seq'), may hold values from 0 to 1023
- frame_count: int32 [16], P('stream'), may hold values from 512 to 2048, as said below
- memory: bfloat16 [2, 16, 512, 512], P(None, 'stream'), may hold values from -6 to 6
- memory_len: int32 [16], P('stream'), may hold values from 0 to 512, as said below
- input_weight: float32 [80, 512], P(None, 'stream'), may hold values from -0.625 to 0.625
- project_weight: float32 [2, 512, 1536], P(None, 'stream'), may hold values from -0.25 to 0.25
- output_weight: float32 [2, 512, 512], P(None, 'stream'), may hold values from -1 to 1
- up_weight: float32 [2, 512, 2048], P(None, 'stream'), may hold values from -0.25 to 0.25
- down_weight: float32 [2, 2048, 512], P(None, 'stream'), may hold values from -0.125 to 0.125
- head_weight: float32 [512, 1024], P('stream'), may hold values from -0.25 to 0.25
- vectors: float32 [11, 512], P(None, 'stream'), may hold values from -1.6 to 2
- slopes: float32 [2, 8], replicated, may hold values from 0.00048828125 to 0.00390625
- first_input: float32 [80, 512], P(None, 'stream'), may hold values from -4.7683716e-07 to 4.7683716e-07
- first_project: float32 [2, 512, 1536], P(None, 'stream'), may hold values from -4.7683716e-07 to 4.7683716e-07
- first_output: float32 [2, 512, 512], P(None, 'stream'), may hold values from -4.7683716e-07 to 4.7683716e-07
- first_up: float32 [2, 512, 2048], P(None, 'stream'), may hold values from -4.7683716e-07 to 4.7683716e-07
- first_down: float32 [2, 2048, 512], P(None, 'stream'), may hold values from -4.7683716e-07 to 4.7683716e-07
- first_head: float32 [512, 1024], P('stream'), may hold values from -4.7683716e-07 to 4.7683716e-07
- first_vectors: float32 [11, 512], P(None, 'stream'), may hold values from -4.7683716e-07 to 4.7683716e-07
- first_slopes: float32 [2, 8], replicated, may hold values from -4.7683716e-07 to 4.7683716e-07
- second_input: float32 [80, 512], P(None, 'stream'), may hold values from 5.8289055e-17 to 2.3315622e-16
- second_project: float32 [2, 512, 1536], P(None, 'stream'), may hold values from 5.8289054e-16 to 2.3315622e-15
- second_output: float32 [2, 512, 512], P(None, 'stream'), may hold values from 5.8289054e-16 to 2.3315622e-15
- second_up: float32 [2, 512, 2048], P(None, 'stream'), may hold values from 5.8289054e-16 to 2.3315622e-15
- second_down: float32 [2, 2048, 512], P(None, 'stream'), may hold values from 5.8289054e-16 to 2.3315622e-15
- second_head: float32 [512, 1024], P('stream'), may hold values from 5.8289054e-16 to 2.3315622e-15
- second_vectors: float32 [11, 512], P(None, 'stream'), may hold values from 5.8289054e-16 to 2.3315622e-15
- second_slopes: float32 [2, 8], replicated, may hold values from 5.8289054e-16 to 2.3315622e-15
Outputs:
- loss: float32 [], replicated
- layer_inputs: bfloat16 [2, 16, 2048, 512], P(None, 'stream', 'seq')
- clip_norm: float32 [], replicated
- norms: float32 [22, 2], replicated
- updated_input: float32 [80, 512], P(None, 'stream')
- updated_project: float32 [2, 512, 1536], P(None, 'stream')
- updated_output: float32 [2, 512, 512], P(None, 'stream')
- updated_up: float32 [2, 512, 2048], P(None, 'stream')
- updated_down: float32 [2, 2048, 512], P(None, 'stream')
- updated_head: float32 [512, 1024], P('stream')
- updated_vectors: float32 [11, 512], P(None, 'stream')
- updated_slopes: float32 [2, 8], replicated
- new_first_input: float32 [80, 512], P(None, 'stream')
- new_first_project: float32 [2, 512, 1536], P(None, 'stream')
- new_first_output: float32 [2, 512, 512], P(None, 'stream')
- new_first_up: float32 [2, 512, 2048], P(None, 'stream')
- new_first_down: float32 [2, 2048, 512], P(None, 'stream')
- new_first_head: float32 [512, 1024], P('stream')
- new_first_vectors: float32 [11, 512], P(None, 'stream')
- new_first_slopes: float32 [2, 8], replicated
- new_second_input: float32 [80, 512], P(None, 'stream')
- new_second_project: float32 [2, 512, 1536], P(None, 'stream')
- new_second_output: float32 [2, 512, 512], P(None, 'stream')
- new_second_up: float32 [2, 512, 2048], P(None, 'stream')
- new_second_down: float32 [2, 2048, 512], P(None, 'stream')
- new_second_head: float32 [512, 1024], P('stream')
- new_second_vectors: float32 [11, 512], P(None, 'stream')
- new_second_slopes: float32 [2, 8], replicated
Inputs may be any that keep to these rules, and one draw needn't show every extreme that they name: Each stream counts its first frame_count frames; some stream counts all 2048. The last memory_len rows of a stream's memory are valid; some stream has all 512, another none.
All inputs are finite; a program needn't handle non-finite values.
Results may differ from a plain program's by a relative error of at most 0.019.
Values may be sent and summed in bfloat16 or wider, within the bound.
A program may use at most 384 MiB of HBM per device.

v0:
```python
import jax
import jax.numpy as jnp
from jax import lax
from jax.sharding import PartitionSpec as P

STEP = 10


ln_eps = 1e-05
clip_limit = 0.002
beta_one = 0.9
beta_two = 0.999
lamb_rate = 0.3
slope_rate = 0.001
decay_rate = 0.01
adam_eps = 1e-11
masked_score = -1e30


def from_behind(block, axis, distance):
    devices = range(lax.axis_size(axis))
    route = [(i - distance, i) for i in devices if i - distance in devices]
    return lax.ppermute(block, axis, route)


def normalize(values):
    centred = values - jnp.mean(values, axis=-1, keepdims=True)
    scale = lax.rsqrt(jnp.mean(centred * centred, axis=-1, keepdims=True) + ln_eps)
    return (centred * scale, scale)


def norm_back(grad_out, standard, scale, gain):
    scaled = grad_out * gain
    return scale * (
        scaled
        - jnp.mean(scaled, axis=-1, keepdims=True)
        - standard * jnp.mean(scaled * standard, axis=-1, keepdims=True)
    )


def gelu_slope(values):
    cumulative = 0.5 * (1.0 + lax.erf(values * 0.7071067811865476))
    density = jnp.exp(-0.5 * values * values) * 0.3989422804014327
    return cumulative + values * density


def scores_of(query, keys, slope, allowed, distance):
    scale = query.shape[-1] ** (-0.5)
    raw = jnp.einsum("sqhd,skhd->shqk", query, keys, preferred_element_type=jnp.float32) * scale
    raw = raw - slope[None, :, None, None] * distance[None, None]
    return jnp.where(allowed[:, None], raw, masked_score)


def attend(query, keys, values, slope, allowed, distance):
    score = scores_of(query, keys, slope, allowed, distance)
    peak = jnp.max(score, axis=-1, keepdims=True)
    exponent = jnp.exp(score - peak)
    total = jnp.sum(exponent, axis=-1, keepdims=True)
    attention = (exponent / total).astype(jnp.bfloat16)
    mixed = jnp.einsum("shqk,skhd->sqhd", attention, values, preferred_element_type=jnp.float32)
    return (mixed, peak + jnp.log(total))


def attend_back(query, keys, values, slope, allowed, distance, log_total, grad_mixed):
    scale = query.shape[-1] ** (-0.5)
    score = scores_of(query, keys, slope, allowed, distance)
    attention = jnp.exp(score - log_total)
    grad_values = jnp.einsum(
        "shqk,sqhd->skhd",
        attention.astype(jnp.bfloat16),
        grad_mixed,
        preferred_element_type=jnp.float32,
    )
    grad_attention = jnp.einsum(
        "sqhd,skhd->shqk", grad_mixed, values, preferred_element_type=jnp.float32
    )
    grad_score = attention * (
        grad_attention - jnp.sum(attention * grad_attention, axis=-1, keepdims=True)
    )
    grad_score = grad_score.astype(jnp.bfloat16)
    grad_slope = -jnp.sum(grad_score.astype(jnp.float32) * distance[None, None], axis=(0, 2, 3))
    grad_query = (
        jnp.einsum("shqk,skhd->sqhd", grad_score, keys, preferred_element_type=jnp.float32) * scale
    )
    grad_keys = (
        jnp.einsum("shqk,sqhd->skhd", grad_score, query, preferred_element_type=jnp.float32) * scale
    )
    return (grad_query, grad_keys, grad_values, grad_slope)


def layer_forward(residual, weights, rows, slope, memory_rows, allowed, distance, first, halo):
    project, output, upward, downward = weights
    gain_one, bias_one, gain_two, bias_two = rows
    streams, span, width = residual.shape
    heads = slope.shape[0]
    head_size = width // heads
    standard_one, scale_one = normalize(residual)
    normed_one = (standard_one * gain_one + bias_one).astype(jnp.bfloat16)
    projected = jnp.einsum(
        "scd,de->sce", normed_one, project, preferred_element_type=jnp.float32
    ).astype(jnp.bfloat16)
    key_value = projected[..., width:]
    standard_mem, unused_scale = normalize(memory_rows.astype(jnp.float32))
    normed_mem = (standard_mem * gain_one + bias_one).astype(jnp.bfloat16)
    memory_kv = jnp.einsum(
        "scd,de->sce", normed_mem, project[:, width:], preferred_element_type=jnp.float32
    ).astype(jnp.bfloat16)
    halo = from_behind(key_value, "seq", 1)
    prior = jnp.where(first, memory_kv, halo)
    joined = jnp.concatenate([prior, key_value], axis=1)
    shape_four = (streams, 2 * span, heads, head_size)
    keys = joined[..., :width].reshape(shape_four)
    values = joined[..., width:].reshape(shape_four)
    query = projected[..., :width].reshape((streams, span, heads, head_size))
    attended, log_total = attend(query, keys, values, slope, allowed, distance)
    mixed = attended.reshape((streams, span, width)).astype(jnp.bfloat16)
    after = residual + jnp.einsum("scd,de->sce", mixed, output, preferred_element_type=jnp.float32)
    standard_two, scale_two = normalize(after)
    normed_two = (standard_two * gain_two + bias_two).astype(jnp.bfloat16)
    hidden = jnp.einsum("scd,df->scf", normed_two, upward, preferred_element_type=jnp.float32)
    active = jax.nn.gelu(hidden, approximate=False).astype(jnp.bfloat16)
    result = after + jnp.einsum("scf,fd->scd", active, downward, preferred_element_type=jnp.float32)
    saved = (
        standard_one,
        scale_one,
        normed_one,
        query,
        keys,
        values,
        standard_mem,
        normed_mem,
        log_total,
        mixed,
        standard_two,
        scale_two,
        normed_two,
        hidden,
        active,
    )
    return (result, halo, saved)


def layer_backward(grad_out, weights, rows, slope, saved, allowed, distance, first):
    project, output, upward, downward = weights
    gain_one, bias_one, gain_two, bias_two = rows
    (
        standard_one,
        scale_one,
        normed_one,
        query,
        keys,
        values,
        standard_mem,
        normed_mem,
        log_total,
        mixed,
        standard_two,
        scale_two,
        normed_two,
        hidden,
        active,
    ) = saved
    streams, span, width = grad_out.shape
    branch_two = grad_out.astype(jnp.bfloat16)
    grad_down = jnp.einsum("scf,scd->fd", active, branch_two, preferred_element_type=jnp.float32)
    grad_active = jnp.einsum(
        "scd,fd->scf", branch_two, downward, preferred_element_type=jnp.float32
    )
    grad_hidden = (grad_active * gelu_slope(hidden)).astype(jnp.bfloat16)
    grad_up = jnp.einsum("scd,scf->df", normed_two, grad_hidden, preferred_element_type=jnp.float32)
    grad_normed_two = jnp.einsum(
        "scf,df->scd", grad_hidden, upward, preferred_element_type=jnp.float32
    )
    grad_gain_two = jnp.sum(grad_normed_two * standard_two, axis=(0, 1))
    grad_bias_two = jnp.sum(grad_normed_two, axis=(0, 1))
    grad_after = grad_out + norm_back(grad_normed_two, standard_two, scale_two, gain_two)
    branch_one = grad_after.astype(jnp.bfloat16)
    grad_output = jnp.einsum("scd,sce->de", mixed, branch_one, preferred_element_type=jnp.float32)
    grad_mixed = jnp.einsum(
        "sce,de->scd", branch_one, output, preferred_element_type=jnp.float32
    ).astype(jnp.bfloat16)
    grad_query, grad_keys, grad_values, grad_slope = attend_back(
        query, keys, values, slope, allowed, distance, log_total, grad_mixed.reshape(query.shape)
    )
    grad_joined = jnp.concatenate(
        [
            grad_keys.reshape((streams, 2 * span, width)),
            grad_values.reshape((streams, 2 * span, width)),
        ],
        axis=-1,
    )
    grad_prior = grad_joined[:, :span]
    returned = from_behind(grad_prior, "seq", -1)
    grad_key_value = grad_joined[:, span:] + returned
    grad_projected = jnp.concatenate(
        [grad_query.reshape((streams, span, width)), grad_key_value], axis=-1
    ).astype(jnp.bfloat16)
    grad_memory = jnp.where(first, grad_prior, 0.0).astype(jnp.bfloat16)
    memory_term = jnp.einsum(
        "scd,sce->de", normed_mem, grad_memory, preferred_element_type=jnp.float32
    )
    grad_project = jnp.einsum(
        "scd,sce->de", normed_one, grad_projected, preferred_element_type=jnp.float32
    )
    grad_project = grad_project + jnp.pad(memory_term, ((0, 0), (width, 0)))
    grad_normed_one = jnp.einsum(
        "sce,de->scd", grad_projected, project, preferred_element_type=jnp.float32
    )
    grad_normed_mem = jnp.einsum(
        "sce,de->scd", grad_memory, project[:, width:], preferred_element_type=jnp.float32
    )
    grad_gain_one = jnp.sum(grad_normed_one * standard_one, axis=(0, 1)) + jnp.sum(
        grad_normed_mem * standard_mem, axis=(0, 1)
    )
    grad_bias_one = jnp.sum(grad_normed_one, axis=(0, 1)) + jnp.sum(grad_normed_mem, axis=(0, 1))
    grad_in = grad_after + norm_back(grad_normed_one, standard_one, scale_one, gain_one)
    row_grads = jnp.stack([grad_gain_one, grad_bias_one, grad_gain_two, grad_bias_two])
    return (grad_in, (grad_project, grad_output, grad_up, grad_down), row_grads, grad_slope)


def per_matrix(arrays):
    parts = [jnp.sum(arrays[0] * arrays[0]).reshape(1)]
    for stacked in arrays[1:5]:
        parts.append(jnp.sum(stacked * stacked, axis=(1, 2)))
    parts.append(jnp.sum(arrays[5] * arrays[5]).reshape(1))
    parts.append(jnp.sum(arrays[6] * arrays[6], axis=1))
    return jnp.concatenate(parts)


def adam_direction(weight, grad, first, second, decay):
    new_first = beta_one * first + (1.0 - beta_one) * grad
    new_second = beta_two * second + (1.0 - beta_two) * grad * grad
    first_hat = new_first / (1.0 - beta_one**STEP)
    second_hat = new_second / (1.0 - beta_two**STEP)
    return (new_first, new_second, first_hat / (jnp.sqrt(second_hat) + adam_eps) + decay * weight)


def shards(
    frames,
    targets,
    frame_count,
    memory,
    memory_len,
    input_weight,
    project_weight,
    output_weight,
    up_weight,
    down_weight,
    head_weight,
    vectors,
    slopes,
    first_input,
    first_project,
    first_output,
    first_up,
    first_down,
    first_head,
    first_vectors,
    first_slopes,
    second_input,
    second_project,
    second_output,
    second_up,
    second_down,
    second_head,
    second_vectors,
    second_slopes,
):
    streams, span, unused_width = frames.shape
    layers = project_weight.shape[0]
    seq_index = lax.axis_index("seq")
    first = seq_index == 0
    streams_all = streams * lax.axis_size("stream")
    gathered = (
        lax.all_gather(input_weight.astype(jnp.bfloat16), "stream", axis=1, tiled=True),
        lax.all_gather(project_weight.astype(jnp.bfloat16), "stream", axis=1, tiled=True),
        lax.all_gather(output_weight.astype(jnp.bfloat16), "stream", axis=1, tiled=True),
        lax.all_gather(up_weight.astype(jnp.bfloat16), "stream", axis=1, tiled=True),
        lax.all_gather(down_weight.astype(jnp.bfloat16), "stream", axis=1, tiled=True),
        lax.all_gather(head_weight.astype(jnp.bfloat16), "stream", axis=0, tiled=True),
        lax.all_gather(vectors.astype(jnp.bfloat16), "stream", axis=1, tiled=True),
    )
    input_low, project_low, output_low, up_low, down_low, head_low, vector_low = gathered
    rows_all = vector_low.astype(jnp.float32)
    query_pos = jnp.arange(span)
    key_pos = jnp.arange(2 * span)
    distance = (query_pos[:, None] + span - key_pos[None]).astype(jnp.float32)
    prior_ok = jnp.logical_or(jnp.logical_not(first), key_pos[None] >= span - memory_len[:, None])
    local_ok = key_pos[None] - span <= query_pos[:, None]
    allowed = jnp.where(key_pos[None, None] < span, prior_ok[:, None, :], local_ok[None])

    def layer_weights(layer):
        return (project_low[layer], output_low[layer], up_low[layer], down_low[layer])

    residual = (
        jnp.einsum("sci,id->scd", frames, input_low, preferred_element_type=jnp.float32)
        + rows_all[0]
    )
    inputs = []
    halos = []
    for layer in range(layers):
        inputs.append(residual)
        residual, halo, unused_saved = layer_forward(
            residual,
            layer_weights(layer),
            rows_all[3 + 4 * layer : 7 + 4 * layer],
            slopes[layer],
            memory[layer],
            allowed,
            distance,
            first,
            None,
        )
        halos.append(halo)
    standard_last, scale_last = normalize(residual)
    normed_last = (standard_last * rows_all[1] + rows_all[2]).astype(jnp.bfloat16)
    logits = jnp.einsum("scd,dv->scv", normed_last, head_low, preferred_element_type=jnp.float32)
    peak = jnp.max(logits, axis=-1, keepdims=True)
    log_total = peak + jnp.log(jnp.sum(jnp.exp(logits - peak), axis=-1, keepdims=True))
    onehot = jnp.arange(logits.shape[-1])[None, None] == targets[..., None]
    picked = jnp.sum(jnp.where(onehot, logits, 0.0), axis=-1)
    position = seq_index * span + jnp.arange(span)
    share = jnp.where(
        position[None] < frame_count[:, None],
        1.0 / (frame_count[:, None].astype(jnp.float32) * streams_all),
        0.0,
    )
    loss_term = jnp.sum(share * (log_total[..., 0] - picked))
    softened = jnp.exp(logits - log_total)
    grad_logits = (share[..., None] * jnp.where(onehot, softened - 1.0, softened)).astype(
        jnp.bfloat16
    )
    grad_head = jnp.einsum(
        "scd,scv->dv", normed_last, grad_logits, preferred_element_type=jnp.float32
    )
    grad_last = jnp.einsum("scv,dv->scd", grad_logits, head_low, preferred_element_type=jnp.float32)
    grad_gain_last = jnp.sum(grad_last * standard_last, axis=(0, 1))
    grad_bias_last = jnp.sum(grad_last, axis=(0, 1))
    grad_residual = norm_back(grad_last, standard_last, scale_last, rows_all[1])
    matrix_grads = [None] * layers
    row_grads = [None] * layers
    slope_grads = [None] * layers
    for layer in reversed(range(layers)):
        rows = rows_all[3 + 4 * layer : 7 + 4 * layer]
        unused_result, unused_halo, saved = layer_forward(
            inputs[layer],
            layer_weights(layer),
            rows,
            slopes[layer],
            memory[layer],
            allowed,
            distance,
            first,
            None,
        )
        grad_residual, matrices, rows_grad, slope_grad = layer_backward(
            grad_residual,
            layer_weights(layer),
            rows,
            slopes[layer],
            saved,
            allowed,
            distance,
            first,
        )
        matrix_grads[layer] = matrices
        row_grads[layer] = rows_grad
        slope_grads[layer] = slope_grad
    grad_input = jnp.einsum(
        "sci,scd->id",
        frames,
        grad_residual.astype(jnp.bfloat16),
        preferred_element_type=jnp.float32,
    )
    leading = jnp.stack([jnp.sum(grad_residual, axis=(0, 1)), grad_gain_last, grad_bias_last])
    grad_rows = jnp.concatenate([leading] + row_grads, axis=0)
    grad_project = jnp.stack([item[0] for item in matrix_grads])
    grad_output = jnp.stack([item[1] for item in matrix_grads])
    grad_up = jnp.stack([item[2] for item in matrix_grads])
    grad_down = jnp.stack([item[3] for item in matrix_grads])
    grad_slopes = jnp.stack(slope_grads)
    grad_input, grad_project, grad_output, grad_up, grad_down, grad_head, grad_rows = (
        lax.psum_scatter(
            grad_input.astype(jnp.bfloat16), "stream", scatter_dimension=1, tiled=True
        ).astype(jnp.float32),
        lax.psum_scatter(
            grad_project.astype(jnp.bfloat16), "stream", scatter_dimension=1, tiled=True
        ).astype(jnp.float32),
        lax.psum_scatter(
            grad_output.astype(jnp.bfloat16), "stream", scatter_dimension=1, tiled=True
        ).astype(jnp.float32),
        lax.psum_scatter(
            grad_up.astype(jnp.bfloat16), "stream", scatter_dimension=1, tiled=True
        ).astype(jnp.float32),
        lax.psum_scatter(
            grad_down.astype(jnp.bfloat16), "stream", scatter_dimension=1, tiled=True
        ).astype(jnp.float32),
        lax.psum_scatter(
            grad_head.astype(jnp.bfloat16), "stream", scatter_dimension=0, tiled=True
        ).astype(jnp.float32),
        lax.psum_scatter(
            grad_rows.astype(jnp.bfloat16), "stream", scatter_dimension=1, tiled=True
        ).astype(jnp.float32),
    )
    grads = (
        lax.psum(grad_input.astype(jnp.bfloat16), "seq").astype(jnp.float32),
        lax.psum(grad_project.astype(jnp.bfloat16), "seq").astype(jnp.float32),
        lax.psum(grad_output.astype(jnp.bfloat16), "seq").astype(jnp.float32),
        lax.psum(grad_up.astype(jnp.bfloat16), "seq").astype(jnp.float32),
        lax.psum(grad_down.astype(jnp.bfloat16), "seq").astype(jnp.float32),
        lax.psum(grad_head.astype(jnp.bfloat16), "seq").astype(jnp.float32),
        lax.psum(grad_rows.astype(jnp.bfloat16), "seq").astype(jnp.float32),
    )
    loss, grad_slopes = lax.psum((loss_term, grad_slopes), ("seq", "stream"))
    grad_squares = lax.psum(per_matrix(grads), "stream")
    clip_norm = jnp.sqrt(jnp.sum(grad_squares) + jnp.sum(grad_slopes * grad_slopes))
    factor = jnp.minimum(1.0, clip_limit / clip_norm)
    weights = (
        input_weight,
        project_weight,
        output_weight,
        up_weight,
        down_weight,
        head_weight,
        vectors,
    )
    firsts = (
        first_input,
        first_project,
        first_output,
        first_up,
        first_down,
        first_head,
        first_vectors,
    )
    seconds = (
        second_input,
        second_project,
        second_output,
        second_up,
        second_down,
        second_head,
        second_vectors,
    )
    moved = [
        adam_direction(
            weights[index], grads[index] * factor, firsts[index], seconds[index], decay_rate
        )
        for index in range(7)
    ]
    updates = [item[2] for item in moved]
    weight_squares, update_squares = lax.psum((per_matrix(weights), per_matrix(updates)), "stream")
    weight_norm = jnp.sqrt(weight_squares)
    update_norm = jnp.sqrt(update_squares)
    ratio = weight_norm / update_norm
    layer_end = 1 + 4 * layers
    shaped = [
        ratio[0],
        ratio[1 : 1 + layers][:, None, None],
        ratio[1 + layers : 1 + 2 * layers][:, None, None],
        ratio[1 + 2 * layers : 1 + 3 * layers][:, None, None],
        ratio[1 + 3 * layers : layer_end][:, None, None],
        ratio[layer_end],
        ratio[layer_end + 1 :][:, None],
    ]
    fresh = [weights[index] - lamb_rate * shaped[index] * updates[index] for index in range(7)]
    slope_first, slope_second, slope_update = adam_direction(
        slopes, grad_slopes * factor, first_slopes, second_slopes, 0.0
    )
    fresh_slopes = slopes - slope_rate * slope_update
    slope_row = jnp.stack(
        [jnp.sqrt(jnp.sum(slopes * slopes)), jnp.sqrt(jnp.sum(slope_update * slope_update))]
    ).reshape((1, 2))
    norms = jnp.concatenate([jnp.stack([weight_norm, update_norm], axis=1), slope_row], axis=0)
    layer_inputs = jnp.stack(inputs).astype(jnp.bfloat16)
    return (
        loss,
        layer_inputs,
        clip_norm,
        norms,
        fresh[0],
        fresh[1],
        fresh[2],
        fresh[3],
        fresh[4],
        fresh[5],
        fresh[6],
        fresh_slopes,
        moved[0][0],
        moved[1][0],
        moved[2][0],
        moved[3][0],
        moved[4][0],
        moved[5][0],
        moved[6][0],
        slope_first,
        moved[0][1],
        moved[1][1],
        moved[2][1],
        moved[3][1],
        moved[4][1],
        moved[5][1],
        moved[6][1],
        slope_second,
    )


def solution(mesh):
    in_specs = (
        P("stream", "seq", None),
        P("stream", "seq"),
        P("stream"),
        P(None, "stream", None, None),
        P("stream"),
        P(None, "stream"),
        P(None, "stream", None),
        P(None, "stream", None),
        P(None, "stream", None),
        P(None, "stream", None),
        P("stream", None),
        P(None, "stream"),
        P(),
        P(None, "stream"),
        P(None, "stream", None),
        P(None, "stream", None),
        P(None, "stream", None),
        P(None, "stream", None),
        P("stream", None),
        P(None, "stream"),
        P(),
        P(None, "stream"),
        P(None, "stream", None),
        P(None, "stream", None),
        P(None, "stream", None),
        P(None, "stream", None),
        P("stream", None),
        P(None, "stream"),
        P(),
    )
    out_specs = (
        P(),
        P(None, "stream", "seq", None),
        P(),
        P(),
        P(None, "stream"),
        P(None, "stream", None),
        P(None, "stream", None),
        P(None, "stream", None),
        P(None, "stream", None),
        P("stream", None),
        P(None, "stream"),
        P(),
        P(None, "stream"),
        P(None, "stream", None),
        P(None, "stream", None),
        P(None, "stream", None),
        P(None, "stream", None),
        P("stream", None),
        P(None, "stream"),
        P(),
        P(None, "stream"),
        P(None, "stream", None),
        P(None, "stream", None),
        P(None, "stream", None),
        P(None, "stream", None),
        P("stream", None),
        P(None, "stream"),
        P(),
    )
    return jax.shard_map(shards, mesh=mesh, in_specs=in_specs, out_specs=out_specs, check_vma=False)
```

profile of v0, /device:TPU:0, one launch (start us, length us, event | category | flops | bytes accessed | tf_op | source)
XLA Modules:
  0.0 1124.1 jit_solution(5709773719585362259)
XLA Ops:
  15.2 10.5 all-gather
  26.5 9.2 all_gather.21
  52.3 5.2 collective-permute-start
  57.6 11.9 %broadcast_multiply_fusion = (f32[8,512,1024]{2,1,0:T(8,128)}, f32[8,512,1024]{2,1,0:T(8,128)}) fusion(f32[8]{0:T(128)S(1)} %get-tuple-element.240, f32[512,1024]{1,0:T(8,128)S(1)} %copy-done.20, f32[8]{0:T(128)S(1)} %get-tuple-element.241), kind=kLoop, calls=%fused_computation.72 | loop fusion | flops 8388608 | bytes 35651648 | tf_op jit(solution)/shard_map/mul | solution.py:50
  87.3 14.1 %collective-permute-done = bf16[2,512,1024]{2,1,0:T(8,128)(2,1)} collective-permute-done((bf16[2,512,1024]{2,1,0:T(8,128)(2,1)}, bf16[2,512,1024]{2,1,0:T(8,128)(2,1)}, u32[]{:S(2)}, u32[]{:S(2)}) %collective-permute-start) | collective-permute-done | bytes 2097184 | tf_op jit(solution)/shard_map/ppermute | solution.py:23
  114.2 20.4 %fusion.194 = (f32[2,8,512]{2,1,0:T(8,128)S(1)}, f32[2,8,512,1024]{3,2,1,0:T(8,128)}) fusion(f32[8,512,1024]{2,1,0:T(8,128)} %get-tuple-element.220, bf16[2,512,8,64]{1,3,2,0:T(8,128)(2,1)} %bitcast.347, bf16[2,1024,8,64]{1,3,2,0:T(8,128)(2,1)} %bitcast.339, pred[2,512,1024]{2,1,0:T(8,128)(4,1)S(1)} %broadcast_select_fusion), kind=kOutput, calls=%fused_computation.430 | convolution fusion | flops 1107288064 | bytes 54558720 | tf_op jit(solution)/shard_map/sqhd,skhd->shqk/dot_general | solution.py:49
  134.7 14.7 %fusion = f32[2,8,512]{2,1,0:T(8,128)S(1)} fusion(f32[2,8,512,1024]{3,2,1,0:T(8,128)} %get-tuple-element.254, f32[2,8,512]{2,1,0:T(8,128)S(1)} %get-tuple-element.253), kind=kLoop, calls=%fused_computation.14 | loop fusion | flops 16769024 | bytes 33619968 | tf_op jit(solution)/shard_map/reduce_sum | solution.py:58
  149.4 13.1 %fusion.99 = bf16[2,8,64,512]{3,2,1,0:T(8,128)(2,1)S(1)} fusion(bf16[2,1024,8,64]{1,3,2,0:T(8,128)(2,1)S(1)} %bitcast.351, f32[2,8,512,1024]{3,2,1,0:T(8,128)} %get-tuple-element.254, f32[2,8,512]{2,1,0:T(8,128)S(1)} %fusion, f32[2,8,512]{2,1,0:T(8,128)S(1)} %get-tuple-element.253), kind=kOutput, calls=%fused_computation.234 | convolution fusion | flops 1099431936 | bytes 36765696 | tf_op jit(solution)/shard_map/shqk,skhd->sqhd/dot_general | solution.py:60
  165.0 7.4 fusion.82
  175.7 19.9 %fusion.14 = bf16[2,512,2048]{2,1,0:T(8,128)(2,1)} fusion(f32[2,512,2048]{2,1,0:T(8,128)S(1)} %get-tuple-element.257, u8[512,2048]{1,0:T(8,128)(4,1)S(1)} %get-tuple-element.143, u8[512,2048]{1,0:T(8,128)(4,1)S(1)} %get-tuple-element.142), kind=kLoop, calls=%fused_computation.30 | loop fusion | flops 146800640 | bytes 14680064 | tf_op jit(solution)/shard_map/convert_element_type | solution.py:121
  195.6 5.4 fusion.196
  205.7 7.5 collective-permute-start.1
  220.3 36.5 %collective-permute-done.1 = bf16[2,512,1024]{2,1,0:T(8,128)(2,1)} collective-permute-done((bf16[2,512,1024]{2,1,0:T(8,128)(2,1)}, bf16[2,512,1024]{2,1,0:T(8,128)(2,1)}, u32[]{:S(2)}, u32[]{:S(2)}) %collective-permute-start.1) | collective-permute-done | bytes 2097184 | tf_op jit(solution)/shard_map/ppermute | solution.py:23
  270.5 20.4 %fusion.197 = (f32[2,8,512]{2,1,0:T(8,128)S(1)}, f32[2,8,512,1024]{3,2,1,0:T(8,128)}) fusion(f32[8,512,1024]{2,1,0:T(8,128)} %get-tuple-element.219, bf16[2,512,8,64]{1,3,2,0:T(8,128)(2,1)} %bitcast.349, bf16[2,1024,8,64]{1,3,2,0:T(8,128)(2,1)S(1)} %bitcast.341, pred[2,512,1024]{2,1,0:T(8,128)(4,1)S(1)} %broadcast_select_fusion), kind=kOutput, calls=%fused_computation.433 | convolution fusion | flops 1107288064 | bytes 54558720 | tf_op jit(solution)/shard_map/sqhd,skhd->shqk/dot_general | solution.py:49
  290.9 14.4 %fusion.1 = f32[2,8,512]{2,1,0:T(8,128)S(1)} fusion(f32[2,8,512,1024]{3,2,1,0:T(8,128)} %get-tuple-element.261, f32[2,8,512]{2,1,0:T(8,128)S(1)} %get-tuple-element.260), kind=kLoop, calls=%fused_computation.15 | loop fusion | flops 16769024 | bytes 33619968 | tf_op jit(solution)/shard_map/reduce_sum | solution.py:58
  305.4 13.7 %fusion.98 = bf16[2,8,64,512]{3,2,1,0:T(8,128)(2,1)S(1)} fusion(bf16[2,1024,8,64]{1,3,2,0:T(8,128)(2,1)S(1)} %bitcast.353, f32[2,8,512,1024]{3,2,1,0:T(8,128)} %get-tuple-element.261, f32[2,8,512]{2,1,0:T(8,128)S(1)} %fusion.1, f32[2,8,512]{2,1,0:T(8,128)S(1)} %get-tuple-element.260), kind=kOutput, calls=%fused_computation.233 | convolution fusion | flops 1099431936 | bytes 36765696 | tf_op jit(solution)/shard_map/shqk,skhd->sqhd/dot_general | solution.py:60
  322.4 5.0 fusion.83
  327.5 19.0 %fusion.17 = bf16[2,512,2048]{2,1,0:T(8,128)(2,1)S(1)} fusion(f32[2,512,2048]{2,1,0:T(8,128)S(1)} %get-tuple-element.264, u8[512,2048]{1,0:T(8,128)(4,1)S(1)} %get-tuple-element.141, u8[512,2048]{1,0:T(8,128)(4,1)S(1)} %get-tuple-element.140), kind=kLoop, calls=%fused_computation.33 | loop fusion | flops 146800640 | bytes 14680064 | tf_op jit(solution)/shard_map/convert_element_type | solution.py:121
  369.0 7.9 fusion.23
  390.1 15.4 %fusion.6 = f32[2,8,64,1024]{3,2,1,0:T(8,128)} fusion(bf16[2,512,8,64]{1,3,2,0:T(8,128)(2,1)S(1)} %bitcast.357, f32[2,8,512,1024]{3,2,1,0:T(8,128)} %get-tuple-element.261, f32[2,8,512]{2,1,0:T(8,128)S(1)} %log_add_fusion.1), kind=kOutput, calls=%fused_computation.19 | convolution fusion | flops 1090519040 | bytes 38830080 | tf_op jit(solution)/shard_map/shqk,sqhd->skhd/dot_general | solution.py:68
  405.6 22.6 %multiply_reduce_fusion.3 = (f32[2,8,512]{2,1,0:T(8,128)S(1)}, f32[2,8,512,1024]{3,2,1,0:T(8,128)}) fusion(f32[2,8,512,1024]{3,2,1,0:T(8,128)} %get-tuple-element.261, f32[2,8,512]{2,1,0:T(8,128)S(1)} %log_add_fusion.1, bf16[2,512,8,64]{1,3,2,0:T(8,128)(2,1)S(1)} %bitcast.358, bf16[2,1024,8,64]{1,3,2,0:T(8,128)(2,1)S(1)} %bitcast.354), kind=kOutput, calls=%fused_computation.6 | convolution fusion | flops 1098899456 | bytes 70320128 | tf_op jit(solution)/shard_map/sqhd,skhd->shqk/dot_general | solution.py:74
  428.1 5.4 copy.279
  433.5 27.8 %multiply_convert_fusion.1 = bf16[2,8,512,1024]{3,2,1,0:T(8,128)(2,1)} fusion(f32[2,8,512,1024]{3,2,1,0:T(8,128)} %get-tuple-element.270, f32[2,8,512,1024]{3,2,1,0:T(8,128)} %get-tuple-element.261, f32[2,8,512]{2,1,0:T(8,128)S(1)} %get-tuple-element.269, f32[2,8,512]{2,1,0:T(8,128)S(1)} %log_add_fusion.1), kind=kLoop, calls=%fused_computation.5 | loop fusion | flops 33554432 | bytes 83951616 | tf_op jit(solution)/shard_map/convert_element_type | solution.py:80
  461.4 10.7 convolution_multiply_fusion.1
  472.1 5.4 copy.278
  486.9 12.6 %multiply_convert_fusion.3 = bf16[2,8,64,512]{3,2,1,0:T(8,128)(2,1)} fusion(bf16[2,1024,8,64]{1,3,2,0:T(8,128)(2,1)} %bitcast.342, bf16[2,8,512,1024]{3,2,1,0:T(8,128)(2,1)} %multiply_convert_fusion.1), kind=kOutput, calls=%fused_computation.176 | convolution fusion | flops 1074790400 | bytes 19922944 | tf_op jit(solution)/shard_map/shqk,skhd->sqhd/dot_general | solution.py:83
  503.8 73.3 %collective-permute-done.2 = f32[2,512,1024]{2,1,0:T(8,128)} collective-permute-done((f32[2,512,1024]{2,1,0:T(8,128)}, f32[2,512,1024]{2,1,0:T(8,128)}, u32[]{:S(2)}, u32[]{:S(2)}) %collective-permute-start.2) | collective-permute-done | bytes 4194336 | tf_op jit(solution)/shard_map/ppermute | solution.py:23
  594.3 7.2 fusion.29
  616.3 5.4 fusion.59
  627.4 6.7 fusion.57
  634.9 15.6 %fusion.4 = f32[2,8,64,1024]{3,2,1,0:T(8,128)} fusion(bf16[2,512,8,64]{1,3,2,0:T(8,128)(2,1)S(1)} %bitcast.355, f32[2,8,512,1024]{3,2,1,0:T(8,128)} %get-tuple-element.254, f32[2,8,512]{2,1,0:T(8,128)S(1)} %log_add_fusion), kind=kOutput, calls=%fused_computation.18 | convolution fusion | flops 1090519040 | bytes 38830080 | tf_op jit(solution)/shard_map/shqk,sqhd->skhd/dot_general | solution.py:68
  650.5 5.6 copy.288
  663.3 23.3 %multiply_reduce_fusion.2 = (f32[2,8,512]{2,1,0:T(8,128)S(1)}, f32[2,8,512,1024]{3,2,1,0:T(8,128)}) fusion(f32[2,8,512,1024]{3,2,1,0:T(8,128)} %get-tuple-element.254, f32[2,8,512]{2,1,0:T(8,128)S(1)} %log_add_fusion, bf16[2,512,8,64]{1,3,2,0:T(8,128)(2,1)S(1)} %bitcast.356, bf16[2,1024,8,64]{1,3,2,0:T(8,128)(2,1)S(1)} %bitcast.352), kind=kOutput, calls=%fused_computation.3 | convolution fusion | flops 1098899456 | bytes 70320128 | tf_op jit(solution)/shard_map/sqhd,skhd->shqk/dot_general | solution.py:74
  688.3 28.6 %multiply_reduce_fusion.1 = (f32[8]{0:T(128)S(1)}, f32[8]{0:T(128)S(1)}, bf16[2,8,512,1024]{3,2,1,0:T(8,128)(2,1)S(1)}) fusion(f32[512,1024]{1,0:T(8,128)S(1)} %copy-done.21, bf16[2,8,512,1024]{3,2,1,0:T(8,128)(2,1)} %multiply_convert_fusion.1, f32[2,8,512,1024]{3,2,1,0:T(8,128)} %get-tuple-element.272, f32[2,8,512]{2,1,0:T(8,128)S(1)} %get-tuple-element.271, ...), kind=kLoop, calls=%fused_computation.1 | loop fusion | flops 83886064 | bytes 102826048 | tf_op jit(solution)/shard_map/reduce_sum | solution.py:81
  716.9 5.6 convolution_multiply_fusion
  725.4 5.4 copy.287
  730.8 5.3 pad_maximum_fusion
  742.5 12.2 %multiply_convert_fusion.2 = bf16[2,8,64,512]{3,2,1,0:T(8,128)(2,1)} fusion(bf16[2,1024,8,64]{1,3,2,0:T(8,128)(2,1)S(1)} %bitcast.340, bf16[2,8,512,1024]{3,2,1,0:T(8,128)(2,1)} %copy-done.1), kind=kOutput, calls=%fused_computation.171 | convolution fusion | flops 1074790400 | bytes 19922944 | tf_op jit(solution)/shard_map/shqk,skhd->sqhd/dot_general | solution.py:83
  763.6 65.4 %collective-permute-done.3 = f32[2,512,1024]{2,1,0:T(8,128)} collective-permute-done((f32[2,512,1024]{2,1,0:T(8,128)}, f32[2,512,1024]{2,1,0:T(8,128)}, u32[]{:S(2)}, u32[]{:S(2)}) %collective-permute-start.3) | collective-permute-done | bytes 4194336 | tf_op jit(solution)/shard_map/ppermute | solution.py:23
  836.5 5.1 fusion.206
  858.4 5.1 fusion.202
  873.6 8.2 reduce-scatter.12.cloned.1.call-done
  884.3 39.6 %all-reduce.2 = (f32[]{:T(128)}, f32[2,8]{1,0:T(2,128)S(1)}) all-reduce(f32[]{:T(128)} %get-tuple-element.208, f32[2,8]{1,0:T(2,128)S(1)} %pad_maximum_fusion.15), channel_id=1, replica_groups=mesh['seq'=4,'stream'=8] {'seq','stream'}, use_global_device_ids=true, to_apply=%region_22.23 | all-reduce | flops 17 | bytes 136 | tf_op jit(solution)/shard_map/psum | solution.py:414
  925.3 30.6 %reduce-scatter.22.cloned.1.call-done = bf16[64,80]{1,0:T(8,128)(2,1)} async-done(((bf16[512,80]{1,0:T(8,128)(2,1)}), bf16[64,80]{1,0:T(8,128)(2,1)}) %reduce-scatter.22.cloned.1.call-update) | async-done | bytes 10256
  956.7 19.4 %all-reduce.4 = (bf16[80,64]{1,0:T(8,128)(2,1)S(1)}, bf16[11,64]{1,0:T(8,128)(2,1)S(1)}) all-reduce(bf16[80,64]{1,0:T(8,128)(2,1)S(1)} %copy.343, bf16[11,64]{1,0:T(8,128)(2,1)S(1)} %copy.345), channel_id=1, replica_groups=mesh['seq'=4,'stream'=8] {'seq'}, use_global_device_ids=true, to_apply=%region_36.37 | all-reduce | flops 5824 | bytes 23296 | tf_op jit(solution)/shard_map/psum | solution.py:406
  976.9 57.4 %all-reduce.8.cloned.1.call-done = (bf16[2,64,1536]{2,1,0:T(8,128)(2,1)}, bf16[2,64,512]{2,1,0:T(8,128)(2,1)}, bf16[2,64,2048]{2,1,0:T(8,128)(2,1)}, bf16[2,256,512]{2,1,0:T(8,128)(2,1)}, bf16[64,1024]{1,0:T(8,128)(2,1)}) async-done(((bf16[2,64,1536]{2,1,0:T(8,128)(2,1)}, bf16[2,64,512]{2,1,0:T(8,128)(2,1)}, bf16[2,64,2048]{2,1,0:T(8,128)(2,1)}, bf16[2,256,512]{2,1,0:T(8,128)(2,1)}, ...) | async-done | bytes 1703952 | tf_op jit(solution)/shard_map/psum | solution.py:407
  1044.1 14.0 %psum.92 = f32[21]{0:T(128)S(1)} all-reduce(f32[21]{0:T(128)} %concatenate.45), channel_id=1, replica_groups=mesh['seq'=4,'stream'=8] {'stream'}, use_global_device_ids=true, to_apply=%region_71.72 | all-reduce | flops 21 | bytes 168 | tf_op jit(solution)/shard_map/psum | solution.py:415
  1085.8 11.8 %all-reduce.3 = (f32[21]{0:T(128)S(1)}, f32[21]{0:T(128)S(1)}) all-reduce(f32[21]{0:T(128)S(1)} %concatenate.47, f32[21]{0:T(128)S(1)} %concatenate.46), channel_id=1, replica_groups=mesh['seq'=4,'stream'=8] {'stream'}, use_global_device_ids=true, to_apply=%region_92.93 | all-reduce | flops 42 | bytes 336 | tf_op jit(solution)/shard_map/psum | solution.py:452
  (571 shorter events, 295.7 us)
Async XLA Ops:
  7.2 29.6 %copy-start = (bf16[2,512,80]{1,2,0:T(8,128)(2,1)S(1)}, bf16[2,512,80]{1,2,0:T(8,128)(2,1)}, u32[]{:S(2)}) copy-start(bf16[2,512,80]{1,2,0:T(8,128)(2,1)} %param.29) | copy-start | bytes 491524
  7.3 38.4 %all-gather.7.cloned.1.call-start = ((), (), s32[]{:S(2)}) async-start(), calls=%async_computation.7 | async-start | bytes 3538944 | tf_op jit(solution)/shard_map/all_gather | solution.py:276
  9.3 62.3 %all-gather.9.cloned.1.call-start = ((), (), s32[]{:S(2)}) async-start(), calls=%async_computation.8 | async-start | bytes 1179648 | tf_op jit(solution)/shard_map/all_gather | solution.py:277
  11.2 153.7 %all-gather.11.cloned.1.call-start = ((), (), s32[]{:S(2)}) async-start(), calls=%async_computation.9 | async-start | bytes 4718592 | tf_op jit(solution)/shard_map/all_gather | solution.py:278
  13.4 182.2 %all-gather.13.cloned.1.call-start = ((), (), s32[]{:S(2)}) async-start(), calls=%async_computation.10 | async-start | bytes 4718592 | tf_op jit(solution)/shard_map/all_gather | solution.py:279
  14.5 336.2 %all-gather.15.cloned.1.call-start = ((), (), s32[]{:S(2)}) async-start(), calls=%async_computation.11 | async-start | bytes 1179648 | tf_op jit(solution)/shard_map/all_gather | solution.py:280
  26.4 74.9 %copy-start.122 = (f32[1,512]{1,0:T(1,128)}, f32[1,512]{1,0:T(1,128)S(1)}, u32[]{:S(2)}) copy-start(f32[1,512]{1,0:T(1,128)S(1)} %get-tuple-element.236) | copy-start | bytes 6148
  26.4 74.9 %copy-start.140 = (f32[1,512]{1,0:T(1,128)}, f32[1,512]{1,0:T(1,128)S(1)}, u32[]{:S(2)}) copy-start(f32[1,512]{1,0:T(1,128)S(1)} %get-tuple-element.235) | copy-start | bytes 6148
  26.4 138.5 %copy-start.124 = (f32[1,512]{1,0:T(1,128)}, f32[1,512]{1,0:T(1,128)S(1)}, u32[]{:S(2)}) copy-start(f32[1,512]{1,0:T(1,128)S(1)} %get-tuple-element.234) | copy-start | bytes 6148
  26.4 138.5 %copy-start.144 = (f32[1,512]{1,0:T(1,128)}, f32[1,512]{1,0:T(1,128)S(1)}, u32[]{:S(2)}) copy-start(f32[1,512]{1,0:T(1,128)S(1)} %get-tuple-element.233) | copy-start | bytes 6148
  26.4 230.3 %copy-start.128 = (f32[1,512]{1,0:T(1,128)}, f32[1,512]{1,0:T(1,128)S(1)}, u32[]{:S(2)}) copy-start(f32[1,512]{1,0:T(1,128)S(1)} %get-tuple-element.232) | copy-start | bytes 6148
  26.5 230.3 %copy-start.142 = (f32[1,512]{1,0:T(1,128)}, f32[1,512]{1,0:T(1,128)S(1)}, u32[]{:S(2)}) copy-start(f32[1,512]{1,0:T(1,128)S(1)} %get-tuple-element.231) | copy-start | bytes 6148
  37.2 125.4 %copy-start.2 = (f32[2,512,512]{1,2,0:T(8,128)}, f32[2,512,512]{1,2,0:T(8,128)S(1)}, u32[]{:S(2)}) copy-start(f32[2,512,512]{1,2,0:T(8,128)S(1)} %get-tuple-element.252) | copy-start | bytes 6291460
  42.2 59.1 %copy-start.112 = (f32[2,512]{1,0:T(2,128)}, f32[2,512]{1,0:T(2,128)S(1)}, u32[]{:S(2)}) copy-start(f32[2,512]{1,0:T(2,128)S(1)} %broadcast_multiply_fusion.18) | copy-start | bytes 12292
  43.0 58.3 %copy-start.130 = (f32[2,512]{1,0:T(2,128)}, f32[2,512]{1,0:T(2,128)S(1)}, u32[]{:S(2)}) copy-start(f32[2,512]{1,0:T(2,128)S(1)} %add_rsqrt_fusion.6) | copy-start | bytes 12292
  52.3 49.0 %collective-permute-start = (bf16[2,512,1024]{2,1,0:T(8,128)(2,1)}, bf16[2,512,1024]{2,1,0:T(8,128)(2,1)}, u32[]{:S(2)}, u32[]{:S(2)}) collective-permute-start(bf16[2,512,1024]{2,1,0:T(8,128)(2,1)} %slice.193), channel_id=1, source_target_pairs={{0,8},{8,16},{16,24},{1,9},{9,17},{17,25},{2,10},{10,18},{18,26},{... | collective-permute-start | bytes 6291464 | tf_op jit(solution)/shard_map/ppermute | solution.py:23
  205.7 51.0 %collective-permute-start.1 = (bf16[2,512,1024]{2,1,0:T(8,128)(2,1)}, bf16[2,512,1024]{2,1,0:T(8,128)(2,1)}, u32[]{:S(2)}, u32[]{:S(2)}) collective-permute-start(bf16[2,512,1024]{2,1,0:T(8,128)(2,1)} %slice.202), channel_id=1, source_target_pairs={{0,8},{8,16},{16,24},{1,9},{9,17},{17,25},{2,10},{10,18},{18,26},{... | collective-permute-start | bytes 6291464 | tf_op jit(solution)/shard_map/ppermute | solution.py:23
  213.9 659.6 %reduce-scatter.20.cloned.1.call-start = ((), (), s32[]{:S(2)}) async-start(), calls=%async_computation.16 | async-start | bytes 1179648 | tf_op jit(solution)/shard_map/reduce_scatter | solution.py:398
  214.8 42.0 %copy-start.33 = (bf16[1,2,512,512]{2,3,1,0:T(8,128)(2,1)}, bf16[1,2,512,512]{2,3,1,0:T(8,128)(2,1)S(1)}, u32[]{:S(2)}) copy-start(bf16[1,2,512,512]{2,3,1,0:T(8,128)(2,1)S(1)} %copy.349) | copy-start | bytes 3145732
  215.0 41.8 %copy-start.114 = (f32[2,512]{1,0:T(2,128)}, f32[2,512]{1,0:T(2,128)S(1)}, u32[]{:S(2)}) copy-start(f32[2,512]{1,0:T(2,128)S(1)} %broadcast_multiply_fusion.15) | copy-start | bytes 12292
  215.3 44.1 %copy-start.132 = (f32[2,512]{1,0:T(2,128)}, f32[2,512]{1,0:T(2,128)S(1)}, u32[]{:S(2)}) copy-start(f32[2,512]{1,0:T(2,128)S(1)} %add_rsqrt_fusion.3) | copy-start | bytes 12292
  319.9 64.2 %copy-start.13 = (f32[2,512,512]{1,2,0:T(8,128)}, f32[2,512,512]{1,2,0:T(8,128)S(1)}, u32[]{:S(2)}) copy-start(f32[2,512,512]{1,2,0:T(8,128)S(1)} %get-tuple-element.263) | copy-start | bytes 6291460
  433.5 27.8 %copy-start.36 = (bf16[2,512,512]{1,2,0:T(8,128)(2,1)S(1)}, bf16[2,512,512]{1,2,0:T(8,128)(2,1)}, u32[]{:S(2)}) copy-start(bf16[2,512,512]{1,2,0:T(8,128)(2,1)} %copy.266) | copy-start | bytes 3145732
  482.4 94.7 %collective-permute-start.2 = (f32[2,512,1024]{2,1,0:T(8,128)}, f32[2,512,1024]{2,1,0:T(8,128)}, u32[]{:S(2)}, u32[]{:S(2)}) collective-permute-start(f32[2,512,1024]{2,1,0:T(8,128)} %pad_maximum_fusion.1), channel_id=1, source_target_pairs={{8,0},{16,8},{24,16},{9,1},{17,9},{25,17},{10,2},{18,10},{26,18},{... | collective-permute-start | bytes 12582920 | tf_op jit(solution)/shard_map/ppermute | solution.py:23
  486.8 386.8 %reduce-scatter.14.cloned.1.call-start = ((), (), s32[]{:S(2)}) async-start(), calls=%async_computation.13 | async-start | bytes 1179648 | tf_op jit(solution)/shard_map/reduce_scatter | solution.py:389
  503.8 77.5 %copy-start.71 = (bf16[2,512,1536]{2,1,0:T(8,128)(2,1)S(1)}, bf16[2,512,1536]{2,1,0:T(8,128)(2,1)}, u32[]{:S(2)}) copy-start(bf16[2,512,1536]{2,1,0:T(8,128)(2,1)} %all-gather.7.cloned.1.call-done) | copy-start | bytes 9437188
  503.8 77.5 %copy-start.91 = (bf16[2,512,512]{2,1,0:T(8,128)(2,1)S(1)}, bf16[2,512,512]{2,1,0:T(8,128)(2,1)}, u32[]{:S(2)}) copy-start(bf16[2,512,512]{2,1,0:T(8,128)(2,1)} %copy.280) | copy-start | bytes 3145732
  616.1 257.5 %reduce-scatter.18.cloned.1.call-start = ((), (), s32[]{:S(2)}) async-start(), calls=%async_computation.15 | async-start | bytes 4718592 | tf_op jit(solution)/shard_map/reduce_scatter | solution.py:395
  626.6 247.0 %reduce-scatter.16.cloned.1.call-start = ((), (), s32[]{:S(2)}) async-start(), calls=%async_computation.14 | async-start | bytes 4718592 | tf_op jit(solution)/shard_map/reduce_scatter | solution.py:392
  686.7 195.1 %reduce-scatter.12.cloned.1.call-start = ((), (), s32[]{:S(2)}) async-start(), calls=%async_computation.12 | async-start | bytes 3538944 | tf_op jit(solution)/shard_map/reduce_scatter | solution.py:386
  688.3 28.6 %copy-start.35 = (bf16[2,512,512]{1,2,0:T(8,128)(2,1)S(1)}, bf16[2,512,512]{1,2,0:T(8,128)(2,1)}, u32[]{:S(2)}) copy-start(bf16[2,512,512]{1,2,0:T(8,128)(2,1)} %copy.255) | copy-start | bytes 3145732
  736.1 92.9 %collective-permute-start.3 = (f32[2,512,1024]{2,1,0:T(8,128)}, f32[2,512,1024]{2,1,0:T(8,128)}, u32[]{:S(2)}, u32[]{:S(2)}) collective-permute-start(f32[2,512,1024]{2,1,0:T(8,128)} %pad_maximum_fusion), channel_id=1, source_target_pairs={{8,0},{16,8},{24,16},{9,1},{17,9},{25,17},{10,2},{18,10},{26,18},{... | collective-permute-start | bytes 12582920 | tf_op jit(solution)/shard_map/ppermute | solution.py:23
  761.6 67.4 %copy-start.4 = (f32[2,1024,512]{2,1,0:T(8,128)S(1)}, f32[2,1024,512]{2,1,0:T(8,128)}, u32[]{:S(2)}) copy-start(f32[2,1024,512]{2,1,0:T(8,128)} %copy.288) | copy-start | bytes 12582916
  761.6 67.4 %copy-start.5 = (f32[2,1024,512]{2,1,0:T(8,128)S(1)}, f32[2,1024,512]{2,1,0:T(8,128)}, u32[]{:S(2)}) copy-start(f32[2,1024,512]{2,1,0:T(8,128)} %copy.287) | copy-start | bytes 12582916
  763.5 68.3 %copy-start.3 = (f32[2,512,512]{1,2,0:T(8,128)S(1)}, f32[2,512,512]{1,2,0:T(8,128)}, u32[]{:S(2)}) copy-start(f32[2,512,512]{1,2,0:T(8,128)} %copy-done.2) | copy-start | bytes 6291460
  763.5 68.3 %copy-start.93 = (bf16[2,512,512]{2,1,0:T(8,128)(2,1)S(1)}, bf16[2,512,512]{2,1,0:T(8,128)(2,1)}, u32[]{:S(2)}) copy-start(bf16[2,512,512]{2,1,0:T(8,128)(2,1)} %copy.289) | copy-start | bytes 3145732
  763.6 68.3 %copy-start.105 = (f32[2,512]{1,0:T(2,128)S(1)}, f32[2,512]{1,0:T(2,128)}, u32[]{:S(2)}) copy-start(f32[2,512]{1,0:T(2,128)} %copy-done.104) | copy-start | bytes 12292
  763.6 68.3 %copy-start.111 = (f32[2,512]{1,0:T(2,128)S(1)}, f32[2,512]{1,0:T(2,128)}, u32[]{:S(2)}) copy-start(f32[2,512]{1,0:T(2,128)} %copy-done.110) | copy-start | bytes 12292
  835.8 88.7 %reduce-scatter.24.cloned.1.call-start = ((), (), s32[]{:S(2)}) async-start(), calls=%async_computation.18 | async-start | bytes 147456
  871.3 171.3 %copy-start.66 = (bf16[1,2,512,512]{2,3,1,0:T(8,128)(2,1)S(1)}, bf16[1,2,512,512]{2,3,1,0:T(8,128)(2,1)}, u32[]{:S(2)}) copy-start(bf16[1,2,512,512]{2,3,1,0:T(8,128)(2,1)} %get-tuple-element.216) | copy-start | bytes 3145732
  871.3 171.3 %copy-start.69 = (bf16[1,2,512,512]{2,3,1,0:T(8,128)(2,1)S(1)}, bf16[1,2,512,512]{2,3,1,0:T(8,128)(2,1)}, u32[]{:S(2)}) copy-start(bf16[1,2,512,512]{2,3,1,0:T(8,128)(2,1)} %get-tuple-element.217) | copy-start | bytes 3145732
  872.2 83.7 %reduce-scatter.22.cloned.1.call-start = ((), (), s32[]{:S(2)}) async-start(), calls=%async_computation.17 | async-start | bytes 147456
  873.5 160.8 %all-reduce.8.cloned.1.call-start = ((), (), s32[]{:S(2)}) async-start(), calls=%async_computation.19 | async-start | bytes 3407872 | tf_op jit(solution)/shard_map/psum | solution.py:407
  881.9 178.2 %copy-start.103 = (f32[11,64]{1,0:T(8,128)S(1)}, f32[11,64]{1,0:T(8,128)}, u32[]{:S(2)}) copy-start(f32[11,64]{1,0:T(8,128)} %param.40) | copy-start | bytes 8452
  882.0 180.1 %copy-start.75 = (f32[64,1024]{1,0:T(8,128)S(1)}, f32[64,1024]{1,0:T(8,128)}, u32[]{:S(2)}) copy-start(f32[64,1024]{1,0:T(8,128)} %param.39) | copy-start | bytes 786436
  923.9 32.0 %copy-start.154 = (f32[2,8]{1,0:T(2,128)}, f32[2,8]{1,0:T(2,128)S(1)}, u32[]{:S(2)}) copy-start(f32[2,8]{1,0:T(2,128)S(1)} %get-tuple-element.176) | copy-start | bytes 196
  1076.9 28.9 %copy-start.120 = (f32[11,64]{1,0:T(8,128)S(1)}, f32[11,64]{1,0:T(8,128)}, u32[]{:S(2)}) copy-start(f32[11,64]{1,0:T(8,128)} %get-tuple-element.190) | copy-start | bytes 8452
  1077.5 28.2 %copy-start.121 = (f32[11,64]{1,0:T(8,128)S(1)}, f32[11,64]{1,0:T(8,128)}, u32[]{:S(2)}) copy-start(f32[11,64]{1,0:T(8,128)} %get-tuple-element.191) | copy-start | bytes 8452
  (138 other events, 974.0 us)
Sparse Core Ops, SparseCore 0:
  10.6 35.0 all-gather.6
  48.1 23.4 all-gather.8
  74.1 36.6 all-gather.10
  113.2 37.4 all-gather.12
  214.1 21.2 all-gather.14
  486.9 40.8 reduce-scatter.19
  616.2 35.5 reduce-scatter.13
  655.1 51.2 reduce-scatter.17
  710.2 51.3 reduce-scatter.15
  836.0 45.8 reduce-scatter.11
  885.7 33.3 reduce-scatter.23
  922.5 33.3 reduce-scatter.21
  958.9 75.3 all-reduce.7
where the time goes:
time: 1130 us; the launch traced here: 1120 us
  matrix products  306 us (27%)
  waiting for transfers between devices  289 us (26%)
  other arithmetic  252 us (22%)
  local copies, waits for them, and re-layouts  135 us (12%)
  blocking collectives  104 us (9%)
  between operations  21.4 us (2%)
  starting transfers between devices  16.8 us (1%)
    ppermute x4, waiting for transfers between devices, from_behind(): return lax.ppermute(block, axis, route)  189 us
    psum x1, waiting for transfers between devices, shards(): lax.psum(grad_project.astype(jnp.bfloat16), 'seq').astype(jnp.float32)  57.4 us
    unnamed x353, local copies, waits for them, and re-layouts  46.2 us
    dot_general x2, matrix products, attend_back(): jnp.einsum('sqhd,skhd->shqk', grad_mixed, values, preferred_element_type=...  45.9 us
    dot_general x2, matrix products, scores_of(): jnp.einsum('sqhd,skhd->shqk', query, keys, preferred_element_type=jnp.flo...  40.9 us
    psum x1, blocking collectives, shards(): loss, grad_slopes = lax.psum((loss_term, grad_slopes), ('seq', 'stream'))  39.6 us
    convert_element_type x2, other arithmetic, layer_forward(): active = jax.nn.gelu(hidden, approximate=False).astype(jnp.bfloat16)  38.9 us
    dot_general x2, matrix products, attend_back(): jnp.einsum('shqk,sqhd->skhd', attention.astype(jnp.bfloat16), grad_mixed,...  31.1 us
  transfers between devices with their start and end apart: 17, of which 9 were waited for; matrix products, arithmetic and copies ran while one was open for 42% of the time, Pallas kernels for 0%

commit v1 on v0

v1 whole, which is shorter than its diff:
```python
import functools

import jax
import jax.numpy as jnp
from jax import lax
from jax.experimental import pallas as pl
from jax.experimental.pallas import tpu as pltpu
from jax.sharding import PartitionSpec as P

STEP = 10


ln_eps = 1e-05
clip_limit = 0.002
beta_one = 0.9
beta_two = 0.999
lamb_rate = 0.3
slope_rate = 0.001
decay_rate = 0.01
adam_eps = 1e-11
masked_score = -1e30

tail_terms = (
    0.16918934881687164,
    0.1706908941268921,
    0.1485215127468109,
    0.21418032050132751,
    -0.09282323718070984,
    0.5449625253677368,
    -0.5097681879997253,
    0.48429951071739197,
    -0.12925273180007935,
)

NN = (((1,), (0,)), ((), ()))
NT = (((1,), (1,)), ((), ()))
TN = (((0,), (0,)), ((), ()))
VMEM_LIMIT = 63 * 1024 * 1024
f32 = jnp.float32
bf16 = jnp.bfloat16


def mm(left, right, dims=NN):
    return lax.dot_general(left, right, dims, preferred_element_type=f32)


def from_behind(block, axis, distance):
    devices = range(lax.axis_size(axis))
    route = [(i - distance, i) for i in devices if i - distance in devices]
    return lax.ppermute(block, axis, route)


def normalize(values):
    centred = values - jnp.mean(values, axis=-1, keepdims=True)
    scale = lax.rsqrt(jnp.mean(centred * centred, axis=-1, keepdims=True) + ln_eps)
    return (centred * scale, scale)


def norm_back(grad_out, standard, scale, gain):
    scaled = grad_out * gain
    return scale * (
        scaled
        - jnp.mean(scaled, axis=-1, keepdims=True)
        - standard * jnp.mean(scaled * standard, axis=-1, keepdims=True)
    )


def gelu_pair(x):
    size = jnp.abs(x)
    t = 1.0 / (1.0 + 0.21213203435596423 * size)
    poly = jnp.full_like(t, tail_terms[-1])
    for term in tail_terms[-2::-1]:
        poly = poly * t + term
    bell = jnp.exp(-0.5 * x * x)
    tail = 0.5 * t * poly * bell
    cumulative = jnp.where(x >= 0.0, 1.0 - tail, tail)
    return (x * cumulative, cumulative + x * (bell * 0.3989422804014327))


def tile(index, size):
    return pl.ds(pl.multiple_of(index * size, size), size)


def half_masks():
    lane = lax.broadcasted_iota(jnp.int32, (1, 128), 1)
    left = jnp.where(lane < 64, 1.0, 0.0).astype(bf16)
    right = jnp.where(lane < 64, 0.0, 1.0).astype(bf16)
    return (left, right)


def attend(streams, span, heads, q_ref, k_ref, v_ref, kf_ref, qf_ref, o_ref, lse_ref):
    pairs = heads // 2
    step = span // 2
    masks = half_masks()
    key_at = lax.broadcasted_iota(jnp.int32, (step, step), 0)
    query_at = lax.broadcasted_iota(jnp.int32, (step, step), 1)

    def one(stream, pair):
        cols = tile(pair, 128)
        k_pair = k_ref[tile(stream, 2 * span), cols]
        v_pair = v_ref[tile(stream, 2 * span), cols]
        outs = []
        for part in range(2):
            done = []
            for half in range(2):
                seen = span + part * step
                q_pair = q_ref[pl.ds(pl.multiple_of(stream * span + part * step, step), step), cols]
                head = 2 * pair + half
                q_aug = q_pair * masks[half] + qf_ref[pl.ds(head, 1), :].astype(bf16)
                k_aug = k_pair[: seen + step] * masks[half] + kf_ref[stream, half, : seen + step]
                v_aug = v_pair[: seen + step] * masks[half] + masks[1 - half]
                wide = mm(k_aug[:seen], q_aug, NT)
                near = mm(k_aug[seen:], q_aug, NT)
                near = jnp.where(key_at <= query_at, near, masked_score)
                peak = jnp.maximum(
                    jnp.max(wide, axis=0, keepdims=True), jnp.max(near, axis=0, keepdims=True)
                )
                wide = jnp.exp(wide - peak).astype(bf16)
                near = jnp.exp(near - peak).astype(bf16)
                mixed = mm(v_aug[:seen], wide, TN) + mm(v_aug[seen:], near, TN)
                own = mixed[half * 64 : half * 64 + 64]
                total = mixed[64 - half * 64 : 128 - half * 64]
                done.append(own / total)
                lse_ref[pl.ds(stream * heads + head, 1), part * step : (part + 1) * step] = (
                    peak + jnp.log(total[:1])
                )
            outs.append(jnp.concatenate(done, axis=0).T)
        for part in range(2):
            o_ref[pl.ds(pl.multiple_of(stream * span + part * step, step), step), cols] = outs[
                part
            ].astype(bf16)

    def over(stream, carry):
        def inner(pair, carry):
            one(stream, pair)
            return carry

        return lax.fori_loop(0, pairs, inner, carry)

    lax.fori_loop(0, streams, over, 0)


def forward_kernel(layer, streams, span, heads, *refs):
    n_in = 12
    if layer == 0:
        (first_ref, rows_ref, frames_ref, halo_ref, small_ref, mem_ref, kf_ref, qf_ref, wp, wo, wu, wd) = refs[:n_in]
        (r_ref, low_ref, pr_ref, a_ref, ap_ref, q_ref, k_ref, v_ref, o_ref, lse_ref, r1_ref, a2_ref, u_ref, gp_ref, out_ref, next_ref) = refs[n_in:]
    else:
        (first_ref, rows_ref, r_ref, a_ref, halo_ref, mem_ref, kf_ref, qf_ref, wp, wo, wu, wd) = refs[:n_in]
        (low_ref, ap_ref, q_ref, k_ref, v_ref, o_ref, lse_ref, r1_ref, a2_ref, u_ref, gp_ref, out_ref) = refs[n_in:]
    width = wp.shape[0]
    first = first_ref[0] > 0
    row = 3 + 4 * layer
    g1, b1, g2, b2 = (rows_ref[row + i : row + i + 1, :] for i in range(4))
    step = span // 2
    for_streams = functools.partial(lax.fori_loop, 0, streams)

    def project(stream, carry):
        for part in range(2):
            at = pl.ds(pl.multiple_of(stream * span + part * step, step), step)
            behind = pl.ds(pl.multiple_of(stream * 2 * span + part * step, step), step)
            here = pl.ds(pl.multiple_of(stream * 2 * span + span + part * step, step), step)
            if layer == 0:
                r = mm(frames_ref[at, :], small_ref[...], NT)
                r_ref[at, :] = r
                low_ref[at, :] = r.astype(bf16)
                a = (normalize(r)[0] * g1 + b1).astype(bf16)
                a_ref[at, :] = a
                before = mm(halo_ref[at, :], small_ref[...], NT)
                before = jnp.where(first, mem_ref[at, :].astype(f32), before)
                pr_ref[at, :] = before
                ap = (normalize(before)[0] * g1 + b1).astype(bf16)
            else:
                low_ref[at, :] = r_ref[at, :].astype(bf16)
                a = a_ref[at, :]
                ap = (normalize(mem_ref[at, :].astype(f32))[0] * g1 + b1).astype(bf16)
                ap = jnp.where(first, ap.astype(f32), halo_ref[at, :].astype(f32)).astype(bf16)
            ap_ref[at, :] = ap
            q_ref[at, :] = (mm(a, wp[:, :width]) * 0.125).astype(bf16)
            k_ref[here, :] = mm(a, wp[:, width : 2 * width]).astype(bf16)
            v_ref[here, :] = mm(a, wp[:, 2 * width :]).astype(bf16)
            k_ref[behind, :] = mm(ap, wp[:, width : 2 * width]).astype(bf16)
            v_ref[behind, :] = mm(ap, wp[:, 2 * width :]).astype(bf16)
        return carry

    for_streams(project, 0)
    attend(streams, span, heads, q_ref, k_ref, v_ref, kf_ref, qf_ref, o_ref, lse_ref)

    def feed(stream, carry):
        at = tile(stream, span)
        after = r_ref[at, :] + mm(o_ref[at, :], wo[...])
        r1_ref[at, :] = after
        a2 = (normalize(after)[0] * g2 + b2).astype(bf16)
        a2_ref[at, :] = a2
        total = after
        for part in range(wu.shape[1] // 512):
            cols = slice(part * 512, (part + 1) * 512)
            active, slope = gelu_pair(mm(a2, wu[:, cols]))
            active = active.astype(bf16)
            u_ref[at, cols] = active
            gp_ref[at, cols] = slope.astype(bf16)
            total = total + mm(active, wd[cols, :])
        out_ref[at, :] = total
        if layer == 0:
            g, b = rows_ref[row + 4 : row + 5, :], rows_ref[row + 5 : row + 6, :]
            next_ref[at, :] = (normalize(total)[0] * g + b).astype(bf16)
        return carry

    for_streams(feed, 0)


def head_kernel(rows_ref, r_ref, wh, target_ref, share_ref, dwh_ref, dr_ref, gr_ref, loss_ref, acc):
    gain, bias = rows_ref[1:2, :], rows_ref[2:3, :]
    step = 256
    acc[...] = jnp.zeros_like(acc)
    gr_ref[...] = jnp.zeros_like(gr_ref)
    loss_ref[...] = jnp.zeros_like(loss_ref)

    def one(index, carry):
        at = tile(index, step)
        standard, scale = normalize(r_ref[at, :])
        f = (standard * gain + bias).astype(bf16)
        z = mm(f, wh[...])
        share = share_ref[at, :]
        peak = jnp.max(z, axis=-1, keepdims=True)
        raised = jnp.exp(z - peak)
        total = jnp.sum(raised, axis=-1, keepdims=True)
        code = lax.broadcasted_iota(jnp.int32, z.shape, 1)
        hit = code == target_ref[at, :]
        picked = jnp.sum(jnp.where(hit, z, 0.0), axis=-1, keepdims=True)
        loss_ref[...] += jnp.sum(share * (peak + jnp.log(total) - picked))
        soft = raised * (1.0 / total)
        dz = (share * jnp.where(hit, soft - 1.0, soft)).astype(bf16)
        acc[...] += mm(f, dz, TN)
        df = mm(dz, wh[...], NT)
        gr_ref[0:1, :] += jnp.sum(df * standard, axis=0, keepdims=True)
        gr_ref[1:2, :] += jnp.sum(df, axis=0, keepdims=True)
        dr_ref[at, :] = norm_back(df, standard, scale, gain)
        return carry

    lax.fori_loop(0, r_ref.shape[0] // step, one, 0)
    dwh_ref[...] = acc[...].astype(bf16)


def attend_back(streams, span, heads, refs):
    (q_ref, k_ref, v_ref, o_ref, lse_ref, kf_ref, qf_ref, do_ref, dq_ref, dk_ref, dv_ref, gs_ref, dk_acc, dv_acc) = refs
    pairs = heads // 2
    step = span // 2
    masks = half_masks()
    key_at = lax.broadcasted_iota(jnp.int32, (step, step), 0)
    query_at = lax.broadcasted_iota(jnp.int32, (step, step), 1)
    head_row = lax.broadcasted_iota(jnp.int32, (8, 128), 0)
    place = lax.broadcasted_iota(jnp.int32, (1, step), 1)
    gs_ref[...] = jnp.zeros_like(gs_ref)

    def one(stream, pair):
        cols = tile(pair, 128)
        k_pair = k_ref[tile(stream, 2 * span), cols]
        v_pair = v_ref[tile(stream, 2 * span), cols]
        dk_acc[...] = jnp.zeros_like(dk_acc)
        dv_acc[...] = jnp.zeros_like(dv_acc)
        for part in range(2):
            seen = span + part * step
            rows = pl.ds(pl.multiple_of(stream * span + part * step, step), step)
            q_pair = q_ref[rows, cols]
            do_pair = do_ref[rows, cols]
            both = (do_pair.astype(f32) * o_ref[rows, cols].astype(f32)).T
            done = []
            for half in range(2):
                head = 2 * pair + half
                mask = masks[half]
                q_own = q_pair * mask
                q_aug = q_own + qf_ref[pl.ds(head, 1), :].astype(bf16)
                k_aug = k_pair[: seen + step] * mask + kf_ref[stream, half, : seen + step]
                do_own = do_pair * mask
                delta = jnp.sum(both[half * 64 : half * 64 + 64], axis=0, keepdims=True)
                log_total = lse_ref[pl.ds(stream * heads + head, 1), part * step : (part + 1) * step]
                turned = jnp.zeros((128, step), f32)
                for low, high in ((0, seen), (seen, seen + step)):
                    score = mm(k_aug[low:high], q_aug, NT)
                    if low:
                        score = jnp.where(key_at <= query_at, score, masked_score)
                    chance = jnp.exp(score - log_total)
                    dp = mm(v_pair[low:high], do_own, NT)
                    dv_acc[low:high, :] += mm(chance.astype(bf16), do_own)
                    ds = (chance * (dp - delta)).astype(bf16)
                    dk_acc[low:high, :] += mm(ds, q_own)
                    turned = turned + mm(k_aug[low:high], ds, TN)
                done.append(turned[half * 64 : half * 64 + 64] * 0.125)
                base = 64 - half * 64
                lean = (
                    turned[base : base + 1]
                    + turned[base + 3 : base + 4]
                    - (place + (part * step + span)).astype(f32) * turned[base + 7 : base + 8]
                )
                gs_ref[...] += jnp.where(head_row == head, jnp.sum(lean), 0.0)
            dq_ref[rows, cols] = jnp.concatenate(done, axis=0).T.astype(bf16)
        dk_ref[tile(stream, 2 * span), cols] = dk_acc[...].astype(bf16)
        dv_ref[tile(stream, 2 * span), cols] = dv_acc[...].astype(bf16)

    def over(stream, carry):
        def inner(pair, carry):
            one(stream, pair)
            return carry

        return lax.fori_loop(0, pairs, inner, carry)

    lax.fori_loop(0, streams, over, 0)


def backward_kernel(layer, streams, span, heads, *refs):
    refs = list(refs)
    (first_ref, rows_ref, a_ref, ap_ref, q_ref, k_ref, v_ref, o_ref, lse_ref, r1_ref, a2_ref, u_ref, gp_ref, kf_ref, qf_ref, wp, wo, wu, wd) = refs[:19]
    rest = refs[19:]
    if layer == 0:
        (frames_ref, halo_ref, r_ref, pr_ref, dr1_in, da_in, back_ref, r_next) = rest[:8]
        (dwp, dwo, dwu, dwd, gr_ref, gs_ref, dsmall_ref) = rest[8:15]
        scratch = rest[15:]
    else:
        (dr_in, mem_ref) = rest[:2]
        (dwp, dwo, dwu, dwd, gr_ref, gs_ref, dr1_out, da_out, dap_out) = rest[2:11]
        scratch = rest[11:]
    (dr_ref, da_ref, do_ref, dq_ref, dk_ref, dv_ref, dk_acc, dv_acc, tr_ref) = scratch
    width = wp.shape[0]
    count = streams * span
    first = first_ref[0] > 0
    row = 3 + 4 * layer
    g1, b1, g2, b2 = (rows_ref[row + i : row + i + 1, :] for i in range(4))
    step = 256
    tiles = count // step
    gr_ref[...] = jnp.zeros_like(gr_ref)

    if layer == 0:
        g = rows_ref[row + 4 : row + 5, :]

        def join(index, carry):
            at = tile(index, step)
            standard, scale = normalize(r_next[at, :])
            da = da_in[at, :] + back_ref[at, :].astype(f32)
            gr_ref[4:5, :] += jnp.sum(da * standard, axis=0, keepdims=True)
            gr_ref[5:6, :] += jnp.sum(da, axis=0, keepdims=True)
            dr_ref[at, :] = dr1_in[at, :] + norm_back(da, standard, scale, g)
            return carry

        lax.fori_loop(0, tiles, join, 0)
    else:

        def take(index, carry):
            at = tile(index, step)
            dr_ref[at, :] = dr_in[at, :]
            return carry

        lax.fori_loop(0, tiles, take, 0)

    da_ref[...] = jnp.zeros_like(da_ref)
    tr_ref[...] = a2_ref[...].T

    def feed(part, carry):
        cols = tile(part, 512)
        dy = dr_ref[...].astype(bf16)
        dh = (mm(dy, wd[cols, :], NT) * gp_ref[:, cols].astype(f32)).astype(bf16)
        dwd[cols, :] = mm(u_ref[:, cols], dy, TN).astype(bf16)
        dwu[:, cols] = mm(tr_ref[...], dh).astype(bf16)
        da_ref[...] += mm(dh, wu[:, cols], NT)
        return carry

    lax.fori_loop(0, wu.shape[1] // 512, feed, 0)

    def middle(index, carry):
        at = tile(index, step)
        standard, scale = normalize(r1_ref[at, :])
        da = da_ref[at, :]
        gr_ref[2:3, :] += jnp.sum(da * standard, axis=0, keepdims=True)
        gr_ref[3:4, :] += jnp.sum(da, axis=0, keepdims=True)
        dr = dr_ref[at, :] + norm_back(da, standard, scale, g2)
        dr_ref[at, :] = dr
        do_ref[at, :] = mm(dr.astype(bf16), wo[...], NT).astype(bf16)
        return carry

    lax.fori_loop(0, tiles, middle, 0)
    dwo[...] = mm(o_ref[...], dr_ref[...].astype(bf16), TN).astype(bf16)

    attend_back(
        streams,
        span,
        heads,
        (q_ref, k_ref, v_ref, o_ref, lse_ref, kf_ref, qf_ref, do_ref, dq_ref, dk_ref, dv_ref, gs_ref, dk_acc, dv_acc),
    )

    tr_ref[...] = a_ref[...].T
    dwp[:, :width] = mm(tr_ref[...], dq_ref[...]).astype(bf16)
    for spot, ref in ((1, dk_ref), (2, dv_ref)):
        total = jnp.zeros((width, width), f32)
        for stream in range(streams):
            behind = slice(stream * 2 * span, stream * 2 * span + span)
            here = slice(stream * 2 * span + span, (stream + 1) * 2 * span)
            own = slice(stream * span, (stream + 1) * span)
            total = total + mm(tr_ref[:, own], ref[here, :])
            total = total + mm(ap_ref[own, :], ref[behind, :], TN)
        dwp[:, spot * width : (spot + 1) * width] = total.astype(bf16)

    if layer == 0:
        dsmall_ref[...] = jnp.zeros_like(dsmall_ref)

    def finish(stream, carry):
        for part in range(span // step):
            at = pl.ds(pl.multiple_of(stream * span + part * step, step), step)
            behind = pl.ds(pl.multiple_of(stream * 2 * span + part * step, step), step)
            here = pl.ds(pl.multiple_of(stream * 2 * span + span + part * step, step), step)
            wq, wk, wv = (wp[:, i * width : (i + 1) * width] for i in range(3))
            da = mm(dq_ref[at, :], wq, NT) + mm(dk_ref[here, :], wk, NT) + mm(dv_ref[here, :], wv, NT)
            dap = mm(dk_ref[behind, :], wk, NT) + mm(dv_ref[behind, :], wv, NT)
            if layer == 0:
                standard, scale = normalize(r_ref[at, :])
                before, before_scale = normalize(pr_ref[at, :])
                gr_ref[0:1, :] += jnp.sum(da * standard + dap * before, axis=0, keepdims=True)
                gr_ref[1:2, :] += jnp.sum(da + dap, axis=0, keepdims=True)
                dr = dr_ref[at, :] + norm_back(da, standard, scale, g1)
                drp = norm_back(dap, before, before_scale, g1)
                drp = jnp.where(first, 0.0, drp)
                gr_ref[6:7, :] += jnp.sum(dr + drp, axis=0, keepdims=True)
                dsmall_ref[...] += mm(dr.astype(bf16), frames_ref[at, :], TN)
                dsmall_ref[...] += mm(drp.astype(bf16), halo_ref[at, :], TN)
            else:
                da_out[at, :] = da
                dr1_out[at, :] = dr_ref[at, :]
                dap_out[at, :] = dap.astype(bf16)
                before, before_scale = normalize(mem_ref[at, :].astype(f32))
                dap = jnp.where(first, dap, 0.0)
                gr_ref[0:1, :] += jnp.sum(dap * before, axis=0, keepdims=True)
                gr_ref[1:2, :] += jnp.sum(dap, axis=0, keepdims=True)
        return carry

    lax.fori_loop(0, streams, finish, 0)


def whole(space=pltpu.VMEM):
    return pl.BlockSpec(memory_space=space)


def call(kernel, name, args, outs, scratch=(), smem=1, flops=0):
    specs = [whole(pltpu.SMEM)] * smem + [whole()] * (len(args) - smem)
    return pl.pallas_call(
        kernel,
        name=name,
        out_shape=[jax.ShapeDtypeStruct(*out) for out in outs],
        in_specs=specs,
        out_specs=[whole()] * len(outs),
        scratch_shapes=[pltpu.VMEM(*item) for item in scratch],
        compiler_params=pltpu.CompilerParams(vmem_limit_bytes=VMEM_LIMIT),
        cost_estimate=pl.CostEstimate(flops=flops, bytes_accessed=20000000, transcendentals=0),
    )(*args)


def split_three(value):
    one = value.astype(bf16)
    rest = value - one.astype(f32)
    two = rest.astype(bf16)
    rest = rest - two.astype(f32)
    return (one, two, rest.astype(bf16))


def per_matrix(arrays):
    parts = [jnp.sum(arrays[0] * arrays[0]).reshape(1)]
    for stacked in arrays[1:5]:
        parts.append(jnp.sum(stacked * stacked, axis=(1, 2)))
    parts.append(jnp.sum(arrays[5] * arrays[5]).reshape(1))
    parts.append(jnp.sum(arrays[6] * arrays[6], axis=1))
    return jnp.concatenate(parts)


def adam_direction(weight, grad, first, second, decay):
    new_first = beta_one * first + (1.0 - beta_one) * grad
    new_second = beta_two * second + (1.0 - beta_two) * grad * grad
    first_hat = new_first / (1.0 - beta_one**STEP)
    second_hat = new_second / (1.0 - beta_two**STEP)
    return (new_first, new_second, first_hat / (jnp.sqrt(second_hat) + adam_eps) + decay * weight)


def shards(
    frames,
    targets,
    frame_count,
    memory,
    memory_len,
    input_weight,
    project_weight,
    output_weight,
    up_weight,
    down_weight,
    head_weight,
    vectors,
    slopes,
    first_input,
    first_project,
    first_output,
    first_up,
    first_down,
    first_head,
    first_vectors,
    first_slopes,
    second_input,
    second_project,
    second_output,
    second_up,
    second_down,
    second_head,
    second_vectors,
    second_slopes,
):
    streams, span, features = frames.shape
    layers, heads = slopes.shape
    nvec = vectors.shape[0]
    width = project_weight.shape[2] // 3
    hidden = up_weight.shape[2]
    codes = head_weight.shape[1]
    count = streams * span
    seq_index = lax.axis_index("seq")
    first = seq_index == 0
    first_flag = jnp.where(first, 1, 0).astype(jnp.int32).reshape(1)
    streams_all = streams * lax.axis_size("stream")

    small_own = jnp.concatenate(
        [input_weight.T, vectors.T, jnp.zeros((input_weight.shape[1], 128 - features - nvec), f32)], axis=1
    ).astype(bf16)
    gather = functools.partial(lax.all_gather, axis_name="stream", tiled=True)
    small = gather(small_own, axis=0)
    weights_low = []
    for layer in range(layers):
        weights_low.append(
            (
                gather(project_weight[layer].astype(bf16), axis=0),
                gather(output_weight[layer].astype(bf16), axis=0),
                gather(up_weight[layer].astype(bf16), axis=0),
                gather(down_weight[layer].astype(bf16), axis=0),
            )
        )
    head_low = gather(head_weight.astype(bf16), axis=0)
    rows = jnp.pad(small[:, features : features + nvec].astype(f32).T, ((0, 16 - nvec), (0, 0)))

    frames_flat = frames.reshape((count, features))
    frames_flat = jnp.concatenate(
        [frames_flat, jnp.ones((count, 1), bf16), jnp.zeros((count, 127 - features), bf16)], axis=1
    )
    frames_behind = from_behind(frames_flat, "seq", 1)
    memory_flat = memory.reshape((layers, count, width))

    key_pos = jnp.arange(2 * span)
    hidden_key = jnp.logical_and(first, key_pos[None] < span - memory_len[:, None])
    coarse = (key_pos // 256 * 256).astype(bf16)
    fine = (key_pos % 256).astype(bf16)
    one = jnp.ones_like(coarse)
    shape = (streams, 2 * span)
    columns = [jnp.broadcast_to(item, shape) for item in (coarse, coarse, coarse, fine, fine, fine)]
    columns += [hidden_key.astype(bf16), jnp.broadcast_to(one, shape)]
    key_marks = jnp.pad(jnp.stack(columns, axis=-1), ((0, 0), (0, 0), (0, 56)))
    blank = jnp.zeros_like(key_marks)
    key_marks = jnp.stack(
        [jnp.concatenate([blank, key_marks], axis=-1), jnp.concatenate([key_marks, blank], axis=-1)], axis=1
    )
    parts = split_three(slopes)
    marks = jnp.stack(parts + parts + (jnp.full_like(parts[0], masked_score), jnp.zeros_like(parts[0])), axis=-1)
    marks = jnp.pad(marks, ((0, 0), (0, 0), (0, 56))).astype(f32)
    even = (jnp.arange(heads) % 2 == 0)[None, :, None]
    query_marks = jnp.concatenate([jnp.where(even, 0.0, marks), jnp.where(even, marks, 0.0)], axis=-1)

    full = ((count, width), f32)
    low = ((count, width), bf16)
    joined = ((2 * count, width), bf16)
    wide = ((count, hidden), bf16)
    lse = ((streams * heads, span), f32)
    saved_outs = [low, low, joined, joined, low, lse, full, low, wide, wide, full]
    cost = 2 * count * (5 * width * width + width * width + 2 * width * hidden) + 4 * count * 2 * span * width

    made = call(
        functools.partial(forward_kernel, 0, streams, span, heads),
        "forward_zero",
        (first_flag, rows, frames_flat, frames_behind, small, memory_flat[0], key_marks, query_marks[0]) + weights_low[0],
        [full, low, full, low] + saved_outs + [low],
        flops=cost,
    )
    r_zero, low_zero, pr_zero, a_zero = made[:4]
    saved_zero = made[4:14]
    r_one, a_one = made[14:16]
    a_behind = from_behind(a_one, "seq", 1)
    made = call(
        functools.partial(forward_kernel, 1, streams, span, heads),
        "forward_one",
        (first_flag, rows, r_one, a_one, a_behind, memory_flat[1], key_marks, query_marks[1]) + weights_low[1],
        [low] + saved_outs,
        flops=cost,
    )
    low_one = made[0]
    saved_one = made[1:11]
    r_two = made[11]

    position = seq_index * span + jnp.arange(span)
    share = jnp.where(
        position[None] < frame_count[:, None],
        1.0 / (frame_count[:, None].astype(f32) * streams_all),
        0.0,
    )
    grad_head, dr_two, last_rows, loss_tile = call(
        head_kernel,
        "head_loss",
        (rows, r_two, head_low, targets.reshape((count, 1)), share.reshape((count, 1))),
        [((width, codes), bf16), full, ((8, width), f32), ((8, 128), f32)],
        [((width, codes), f32)],
        smem=0,
        flops=6 * count * width * codes,
    )
    loss_term = loss_tile[0, 0]

    weight_outs = [
        ((width, 3 * width), bf16),
        ((width, width), bf16),
        ((width, hidden), bf16),
        ((hidden, width), bf16),
        ((8, width), f32),
        ((8, 128), f32),
    ]
    scratch = [full, full, low, low, joined, joined, ((2 * span, 128), f32), ((2 * span, 128), f32), ((width, count), bf16)]
    made = call(
        functools.partial(backward_kernel, 1, streams, span, heads),
        "backward_one",
        (first_flag, rows, a_one, *saved_one[:9], saved_one[9], key_marks, query_marks[1], *weights_low[1], dr_two, memory_flat[1]),
        weight_outs + [full, full, low],
        scratch,
        flops=2 * cost,
    )
    matrices_one, rows_one, slope_one = made[:4], made[4], made[5]
    dr1_one, da_one, dap_one = made[6:]
    back_one = from_behind(dap_one, "seq", -1)
    made = call(
        functools.partial(backward_kernel, 0, streams, span, heads),
        "backward_zero",
        (first_flag, rows, a_zero, *saved_zero[:9], saved_zero[9], key_marks, query_marks[0], *weights_low[0], frames_flat, frames_behind, r_zero, pr_zero, dr1_one, da_one, back_one, r_one),
        weight_outs + [((width, 128), f32)],
        scratch,
        flops=2 * cost,
    )
    matrices_zero, rows_zero, slope_zero, grad_small = made[:4], made[4], made[5], made[6]

    grad_rows = jnp.concatenate(
        [rows_zero[6:7], last_rows[0:2], rows_zero[0:4], rows_one[0:2] + rows_zero[4:6], rows_one[2:4]], axis=0
    )
    grad_slopes = jnp.stack([slope_zero[:, 0], slope_one[:, 0]])
    grad_small = jnp.concatenate(
        [grad_small[:, :features], grad_rows.T, jnp.zeros((width, 128 - features - nvec), f32)], axis=1
    ).astype(bf16)

    def scatter(grad):
        return lax.psum_scatter(grad, "stream", scatter_dimension=0, tiled=True)

    head_share = scatter(grad_head)
    one_share = [scatter(item) for item in matrices_one]
    zero_share = [scatter(item) for item in matrices_zero]
    small_share = scatter(grad_small)
    head_share, one_share, zero_share, small_share = lax.psum(
        (head_share, one_share, zero_share, small_share), "seq"
    )
    pairs_of = [jnp.stack([zero, one]).astype(f32) for zero, one in zip(zero_share, one_share)]
    small_share = small_share.astype(f32)
    grads = (
        small_share[:, :features].T,
        pairs_of[0],
        pairs_of[1],
        pairs_of[2],
        pairs_of[3],
        head_share.astype(f32),
        small_share[:, features : features + nvec].T,
    )
    loss, grad_slopes = lax.psum((loss_term, grad_slopes), ("seq", "stream"))
    grad_squares = lax.psum(per_matrix(grads), "stream")
    clip_norm = jnp.sqrt(jnp.sum(grad_squares) + jnp.sum(grad_slopes * grad_slopes))
    factor = jnp.minimum(1.0, clip_limit / clip_norm)
    weights = (
        input_weight,
        project_weight,
        output_weight,
        up_weight,
        down_weight,
        head_weight,
        vectors,
    )
    firsts = (
        first_input,
        first_project,
        first_output,
        first_up,
        first_down,
        first_head,
        first_vectors,
    )
    seconds = (
        second_input,
        second_project,
        second_output,
        second_up,
        second_down,
        second_head,
        second_vectors,
    )
    moved = [
        adam_direction(
            weights[index], grads[index] * factor, firsts[index], seconds[index], decay_rate
        )
        for index in range(7)
    ]
    updates = [item[2] for item in moved]
    weight_squares, update_squares = lax.psum((per_matrix(weights), per_matrix(updates)), "stream")
    weight_norm = jnp.sqrt(weight_squares)
    update_norm = jnp.sqrt(update_squares)
    ratio = weight_norm / update_norm
    layer_end = 1 + 4 * layers
    shaped = [
        ratio[0],
        ratio[1 : 1 + layers][:, None, None],
        ratio[1 + layers : 1 + 2 * layers][:, None, None],
        ratio[1 + 2 * layers : 1 + 3 * layers][:, None, None],
        ratio[1 + 3 * layers : layer_end][:, None, None],
        ratio[layer_end],
        ratio[layer_end + 1 :][:, None],
    ]
    fresh = [weights[index] - lamb_rate * shaped[index] * updates[index] for index in range(7)]
    slope_first, slope_second, slope_update = adam_direction(
        slopes, grad_slopes * factor, first_slopes, second_slopes, 0.0
    )
    fresh_slopes = slopes - slope_rate * slope_update
    slope_row = jnp.stack(
        [jnp.sqrt(jnp.sum(slopes * slopes)), jnp.sqrt(jnp.sum(slope_update * slope_update))]
    ).reshape((1, 2))
    norms = jnp.concatenate([jnp.stack([weight_norm, update_norm], axis=1), slope_row], axis=0)
    layer_inputs = jnp.stack([low_zero, low_one]).reshape((layers, streams, span, width))
    return (
        loss,
        layer_inputs,
        clip_norm,
        norms,
        *fresh,
        fresh_slopes,
        *[item[0] for item in moved],
        slope_first,
        *[item[1] for item in moved],
        slope_second,
    )


def solution(mesh):
    rows3 = P(None, "stream", None)
    state = (P(None, "stream"), rows3, rows3, rows3, rows3, P("stream", None), P(None, "stream"), P())
    in_specs = (
        P("stream", "seq", None),
        P("stream", "seq"),
        P("stream"),
        P(None, "stream", None, None),
        P("stream"),
    ) + state * 3
    out_specs = (P(), P(None, "stream", "seq", None), P(), P()) + state * 3
    return jax.shard_map(shards, mesh=mesh, in_specs=in_specs, out_specs=out_specs, check_vma=False)
```

time: 1130 us -> 896 us (0.79)
  matrix products: 306 us -> 0 us
  Pallas kernels: 0 us -> 222 us
  other arithmetic: 252 us -> 48.7 us
  waiting for transfers between devices: 289 us -> 449 us
  local copies, waits for them, and re-layouts: 135 us -> 24.1 us
  blocking collectives: 104 us -> 116 us
    dot_general x47 -> x0, matrix products: 306 us -> none  [the longest x2 45.9 us: attend_back(): jnp.einsum('sqhd,skhd->shqk', grad_mixed, values, preferred_element_type=...]
    reduce_scatter x5 -> x10, waiting for transfers between devices: 8.28 us -> 288 us  [scatter(): return lax.psum_scatter(grad, 'stream', scatter_dimension=0, tiled=True)]
    pallas_call x0 -> x5, Pallas kernels: none -> 222 us  [call(): pl.pallas_call(kernel, name=name, out_shape=[jax.ShapeDtypeStruct(*out) f...]
    ppermute x4 -> x3, waiting for transfers between devices: 189 us -> 25.4 us  [from_behind(): return lax.ppermute(block, axis, route)]
    reduce_sum x22 -> x1, other arithmetic: 84.4 us -> 0.6 us  [shards(): jnp.sum(slopes * slopes)]
    all_gather x5 -> x7, waiting for transfers between devices: 3.22 us -> 76.4 us  [the longest x2 52.6 us: shards(): gather(down_weight[layer].astype(bf16), axis=0)]
    convert_element_type x8 -> x5, other arithmetic: 73 us -> 0.77 us  [the longest x1 0.67 us: shards(): head_low = gather(head_weight.astype(bf16), axis=0)]
    unnamed x353 -> x124, local copies, waits for them, and re-layouts: 46.2 us -> 6.97 us
  transfers between devices with their start and end apart: 17 -> 21, of which waited for: 9 -> 12; matrix products, arithmetic and copies ran while one was open for 42% -> 2% of each run, Pallas kernels for 0% -> 17%
where the time goes in v1:
time: 896 us; the launch traced here: 892 us
  waiting for transfers between devices  449 us (50%)
  Pallas kernels  222 us (25%)
  blocking collectives  116 us (13%)
  other arithmetic  48.7 us (5%)
  local copies, waits for them, and re-layouts  24.1 us (3%)
  between operations  20.4 us (2%)
  starting transfers between devices  11.5 us (1%)
    reduce_scatter x10, waiting for transfers between devices, scatter(): return lax.psum_scatter(grad, 'stream', scatter_dimension=0, tiled=True)  288 us
    pallas_call x5, Pallas kernels, call(): pl.pallas_call(kernel, name=name, out_shape=[jax.ShapeDtypeStruct(*out) f...  222 us
    psum x1, waiting for transfers between devices, shards(): lax.psum((head_share, one_share, zero_share, small_share), 'seq')  53.6 us
    all_gather x2, waiting for transfers between devices, shards(): gather(down_weight[layer].astype(bf16), axis=0)  52.6 us
    psum x1, blocking collectives, shards(): loss, grad_slopes = lax.psum((loss_term, grad_slopes), ('seq', 'stream'))  39.8 us
    ppermute x3, waiting for transfers between devices, from_behind(): return lax.ppermute(block, axis, route)  25.4 us
    all_gather x2, waiting for transfers between devices, shards(): gather(up_weight[layer].astype(bf16), axis=0)  23.8 us
    all_gather x2, blocking collectives, shards(): gather(output_weight[layer].astype(bf16), axis=0)  22.4 us
  transfers between devices with their start and end apart: 21, of which 12 were waited for; matrix products, arithmetic and copies ran while one was open for 2% of the time, Pallas kernels for 17%

profile of v1, /device:TPU:0, one launch (start us, length us, event | category | flops | bytes accessed | tf_op | source)
XLA Modules:
  0.0 892.0 jit_solution(1765943122531766867)
XLA Ops:
  13.0 4.9 collective-permute-start
  19.0 9.2 %all_gather.30.refs_4_ = bf16[512,128]{1,0:T(8,128)(2,1)S(1)} all-gather(bf16[64,128]{1,0:T(8,128)(2,1)S(1)} %maximum_maximum_fusion.2), channel_id=1, replica_groups=mesh['seq'=4,'stream'=8] {'stream'}, dimensions={0}, use_global_device_ids=true | all-gather | bytes 147456 | tf_op jit(solution)/shard_map/all_gather | solution.py:527
  32.2 11.6 %all-gather.1 = bf16[1,512,512]{2,1,0:T(8,128)(2,1)} all-gather(bf16[1,64,512]{2,1,0:T(8,128)(2,1)S(1)} %get-tuple-element.291), channel_id=3, replica_groups=mesh['seq'=4,'stream'=8] {'stream'}, dimensions={1}, use_global_device_ids=true | all-gather | bytes 589824 | tf_op jit(solution)/shard_map/all_gather | solution.py:533
  45.2 1.4 fusion.58
  46.6 23.8 %all-gather.20.cloned.1.call-done = bf16[1,512,2048]{2,1,0:T(8,128)(2,1)} async-done(((bf16[1,64,2048]{2,1,0:T(8,128)(2,1)}), bf16[1,512,2048]{2,1,0:T(8,128)(2,1)}) %all-gather.20.cloned.1.call-update) | async-done | bytes 2097168 | tf_op jit(solution)/shard_map/all_gather | solution.py:534
  70.4 30.4 %all-gather.22.cloned.1.call-done = bf16[1,2048,512]{2,1,0:T(8,128)(2,1)} async-done(((bf16[1,256,512]{2,1,0:T(8,128)(2,1)}), bf16[1,2048,512]{2,1,0:T(8,128)(2,1)}) %all-gather.22.cloned.1.call-update) | async-done | bytes 2097168 | tf_op jit(solution)/shard_map/all_gather | solution.py:535
  100.8 48.0 %forward_zero.1 = (f32[1024,512]{1,0:T(8,128)}, bf16[1024,512]{1,0:T(8,128)(2,1)}, f32[1024,512]{1,0:T(8,128)}, bf16[1024,512]{1,0:T(8,128)(2,1)}, bf16[1024,512...) custom-call(s32[1]{0:T(128)} %bitcast.3.refs_0_, ...), custom_call_target="tpu_custom_call" | custom-call | flops 9663676416 | bytes 20000000 | tf_op jit(solution)/shard_map/forward_zero/pallas_call | solution.py:443
  148.9 4.4 collective-permute-start.1
  156.4 10.8 %all-gather.5 = bf16[1,512,512]{2,1,0:T(8,128)(2,1)} all-gather(bf16[1,64,512]{2,1,0:T(8,128)(2,1)S(1)} %copy-done.32), channel_id=7, replica_groups=mesh['seq'=4,'stream'=8] {'stream'}, dimensions={1}, use_global_device_ids=true | all-gather | bytes 589824 | tf_op jit(solution)/shard_map/all_gather | solution.py:533
  167.1 22.2 %all-gather.28.cloned.1.call-done = bf16[1,2048,512]{2,1,0:T(8,128)(2,1)} async-done(((bf16[1,256,512]{2,1,0:T(8,128)(2,1)}), bf16[1,2048,512]{2,1,0:T(8,128)(2,1)}) %all-gather.28.cloned.1.call-update) | async-done | bytes 2097168 | tf_op jit(solution)/shard_map/all_gather | solution.py:535
  189.3 44.0 %forward_one.1 = (bf16[1024,512]{1,0:T(8,128)(2,1)}, bf16[1024,512]{1,0:T(8,128)(2,1)}, bf16[1024,512]{1,0:T(8,128)(2,1)}, bf16[2048,512]{1,0:T(8,128)(2,1)}, bf...) custom-call(s32[1]{0:T(128)} %bitcast.3.refs_0_, ...), custom_call_target="tpu_custom_call" | custom-call | flops 9663676416 | bytes 20000000 | tf_op jit(solution)/shard_map/forward_one/pallas_call | solution.py:443
  233.4 11.2 %head_loss.1 = (bf16[512,1024]{1,0:T(8,128)(2,1)}, f32[1024,512]{1,0:T(8,128)}, f32[8,512]{1,0:T(8,128)}, f32[8,128]{1,0:T(8,128)}) custom-call(f32[16,512]{1,0:T(8,128)} %pad_convert_fusion.refs_1_.rows_ref, f32[1024,512]{1,0:T(8,128)} %get-tuple-element.78.r_ref, bf16[512,1024]{1,0:T(8,128)(2,1)} %all-gather.16.cloned.1.call-done.wh, s32[1024,1]{1,0:T(8,128)} %bitcast.97, ...), custom_call_target="tpu_custom_call" | custom-call | flops 3221225472 | bytes 20000000 | tf_op jit(solution)/shard_map/head_loss/pallas_call | solution.py:443
  244.6 57.1 %backward_one.1 = (bf16[512,1536]{1,0:T(8,128)(2,1)}, bf16[512,512]{1,0:T(8,128)(2,1)}, bf16[512,2048]{1,0:T(8,128)(2,1)}, bf16[2048,512]{1,0:T(8,128)(2,1)}, f3...) custom-call(s32[1]{0:T(128)} %bitcast.3.refs_0_, ...), custom_call_target="tpu_custom_call" | custom-call | flops 19327352832 | bytes 20000000 | tf_op jit(solution)/shard_map/backward_one/pallas_call | solution.py:443
  301.7 1.3 collective-permute-start.2
  303.8 25.4 %collective-permute-done.2.refs_25_ = bf16[1024,512]{1,0:T(8,128)(2,1)} collective-permute-done((bf16[1024,512]{1,0:T(8,128)(2,1)}, bf16[1024,512]{1,0:T(8,128)(2,1)}, u32[]{:S(2)}, u32[]{:S(2)}) %collective-permute-start.2) | collective-permute-done | bytes 1048608 | tf_op jit(solution)/shard_map/ppermute | solution.py:50
  329.2 61.9 %backward_zero.1 = (bf16[512,1536]{1,0:T(8,128)(2,1)}, bf16[512,512]{1,0:T(8,128)(2,1)}, bf16[512,2048]{1,0:T(8,128)(2,1)}, bf16[2048,512]{1,0:T(8,128)(2,1)}, f...) custom-call(s32[1]{0:T(128)} %bitcast.3.refs_0_, f32[16,512]{1,0:T(8,128)} %pad_convert_fusion.refs_1_.rows_ref, ...), custom_call_target="tpu_custom_call" | custom-call | flops 19327352832 | bytes 20000000 | tf_op jit(solution)/shard_map/backward_zero/pallas_call | solution.py:443
  398.4 26.1 %reduce-scatter.17.cloned.1.call-done = bf16[64,512]{1,0:T(8,128)(2,1)} async-done(((bf16[512,512]{1,0:T(8,128)(2,1)}), bf16[64,512]{1,0:T(8,128)(2,1)}) %reduce-scatter.17.cloned.1.call-update) | async-done | bytes 65552 | tf_op jit(solution)/shard_map/reduce_scatter | solution.py:653
  424.5 41.8 %reduce-scatter.15.cloned.1.call-done = bf16[64,1536]{1,0:T(8,128)(2,1)} async-done(((bf16[512,1536]{1,0:T(8,128)(2,1)}), bf16[64,1536]{1,0:T(8,128)(2,1)}) %reduce-scatter.15.cloned.1.call-update) | async-done | bytes 196624 | tf_op jit(solution)/shard_map/reduce_scatter | solution.py:653
  466.3 44.4 %reduce-scatter.23.cloned.1.call-done = bf16[64,2048]{1,0:T(8,128)(2,1)} async-done(((bf16[512,2048]{1,0:T(8,128)(2,1)}), bf16[64,2048]{1,0:T(8,128)(2,1)}) %reduce-scatter.23.cloned.1.call-update) | async-done | bytes 262160 | tf_op jit(solution)/shard_map/reduce_scatter | solution.py:653
  510.7 44.9 %reduce-scatter.27.cloned.1.call-done = bf16[256,512]{1,0:T(8,128)(2,1)} async-done(((bf16[2048,512]{1,0:T(8,128)(2,1)}), bf16[256,512]{1,0:T(8,128)(2,1)}) %reduce-scatter.27.cloned.1.call-update) | async-done | bytes 262160 | tf_op jit(solution)/shard_map/reduce_scatter | solution.py:653
  555.6 41.7 %reduce-scatter.13.cloned.1.call-done = bf16[64,1536]{1,0:T(8,128)(2,1)} async-done(((bf16[512,1536]{1,0:T(8,128)(2,1)}), bf16[64,1536]{1,0:T(8,128)(2,1)}) %reduce-scatter.13.cloned.1.call-update) | async-done | bytes 196624 | tf_op jit(solution)/shard_map/reduce_scatter | solution.py:653
  597.2 44.3 %reduce-scatter.21.cloned.1.call-done = bf16[64,2048]{1,0:T(8,128)(2,1)} async-done(((bf16[512,2048]{1,0:T(8,128)(2,1)}), bf16[64,2048]{1,0:T(8,128)(2,1)}) %reduce-scatter.21.cloned.1.call-update) | async-done | bytes 262160 | tf_op jit(solution)/shard_map/reduce_scatter | solution.py:653
  641.6 44.7 %reduce-scatter.25.cloned.1.call-done = bf16[256,512]{1,0:T(8,128)(2,1)} async-done(((bf16[2048,512]{1,0:T(8,128)(2,1)}), bf16[256,512]{1,0:T(8,128)(2,1)}) %reduce-scatter.25.cloned.1.call-update) | async-done | bytes 262160 | tf_op jit(solution)/shard_map/reduce_scatter | solution.py:653
  690.0 39.8 %all-reduce.5 = (f32[]{:T(128)}, f32[2,8]{1,0:T(2,128)S(1)}) all-reduce(f32[]{:T(128)} %bitcast.23, f32[2,8]{1,0:T(2,128)S(1)} %pad_maximum_fusion.7), channel_id=1, replica_groups=mesh['seq'=4,'stream'=8] {'seq','stream'}, use_global_device_ids=true, to_apply=%region_0.1 | all-reduce | flops 17 | bytes 136 | tf_op jit(solution)/shard_map/psum | solution.py:673
  729.8 19.4 %psum.106 = bf16[64,128]{1,0:T(8,128)(2,1)S(1)} all-reduce(bf16[64,128]{1,0:T(8,128)(2,1)} %reduce-scatter.11.cloned.1.call-done), channel_id=1, replica_groups=mesh['seq'=4,'stream'=8] {'seq'}, use_global_device_ids=true, to_apply=%region_2.3 | all-reduce | flops 8192 | bytes 32768 | tf_op jit(solution)/shard_map/psum | solution.py:659
  749.9 53.6 %all-reduce.10.cloned.1.call-done = (bf16[1,64,1536]{2,1,0:T(8,128)(2,1)}, bf16[1,64,1536]{2,1,0:T(8,128)(2,1)}, bf16[1,64,512]{2,1,0:T(8,128)(2,1)}, bf16[1,64,...) async-done(((bf16[1,64,1536]{2,1,0:T(8,128)(2,1)}, ...) | async-done | bytes 1703952 | tf_op jit(solution)/shard_map/psum | solution.py:659
  803.5 1.6 fusion.17
  807.3 1.3 fusion.4
  808.6 1.3 fusion.5
  809.8 1.4 concatenate.44
  811.8 13.6 %psum.116 = f32[21]{0:T(128)S(1)} all-reduce(f32[21]{0:T(128)S(1)} %concatenate.44), channel_id=1, replica_groups=mesh['seq'=4,'stream'=8] {'stream'}, use_global_device_ids=true, to_apply=%region_28.29 | all-reduce | flops 21 | bytes 168 | tf_op jit(solution)/shard_map/psum | solution.py:674
  828.8 3.3 multiply_reduce_fusion.5
  832.1 1.5 multiply_reduce_fusion.9
  833.8 2.8 multiply_reduce_fusion.3
  836.6 2.8 multiply_reduce_fusion.2
  839.4 1.6 multiply_reduce_fusion.8
  841.6 2.5 concatenate.46
  844.1 2.6 concatenate.45
  846.7 3.1 pad_maximum_fusion
  849.8 11.9 %all-reduce.6 = (f32[21]{0:T(128)S(1)}, f32[21]{0:T(128)S(1)}) all-reduce(f32[21]{0:T(128)S(1)} %copy-done.53, f32[21]{0:T(128)} %concatenate.45), channel_id=1, replica_groups=mesh['seq'=4,'stream'=8] {'stream'}, use_global_device_ids=true, to_apply=%region_47.48 | all-reduce | flops 42 | bytes 336 | tf_op jit(solution)/shard_map/psum | solution.py:711
  864.0 1.3 multiply_subtract_fusion.7
  870.5 1.3 multiply_subtract_fusion.5
  871.8 1.4 copy.147
  873.3 1.4 pad_maximum_fusion.8
  874.6 1.4 multiply_subtract_fusion.6
  876.1 2.8 multiply_subtract_fusion.2
  879.8 1.5 multiply_subtract_fusion.1
  881.4 1.5 multiply_subtract_fusion
  (246 shorter events, 39.3 us)
Async XLA Ops:
  7.2 39.4 %all-gather.18.cloned.1.call-start = ((), (), s32[]{:S(2)}) async-start(), calls=%async_computation.21 | async-start | bytes 1769472 | tf_op jit(solution)/shard_map/all_gather | solution.py:532
  9.3 61.1 %all-gather.20.cloned.1.call-start = ((), (), s32[]{:S(2)}) async-start(), calls=%async_computation.22 | async-start | bytes 2359296 | tf_op jit(solution)/shard_map/all_gather | solution.py:534
  10.3 7.7 copy-start.41
  10.3 8.6 copy-start.27
  10.3 90.5 %all-gather.22.cloned.1.call-start = ((), (), s32[]{:S(2)}) async-start(), calls=%async_computation.23 | async-start | bytes 2359296 | tf_op jit(solution)/shard_map/all_gather | solution.py:535
  10.5 18.0 %copy-start.55 = (s32[2]{0:T(128)S(1)}, s32[2]{0:T(128)}, u32[]{:S(2)}) copy-start(s32[2]{0:T(128)} %param.33) | copy-start | bytes 28
  11.3 17.8 %copy-start.47 = (f32[2,8]{1,0:T(2,128)S(1)}, f32[2,8]{1,0:T(2,128)}, u32[]{:S(2)}) copy-start(f32[2,8]{1,0:T(2,128)} %param.41) | copy-start | bytes 196
  11.4 18.7 %copy-start.9 = (f32[2,64,512]{2,1,0:T(8,128)S(1)}, f32[2,64,512]{2,1,0:T(8,128)}, u32[]{:S(2)}) copy-start(f32[2,64,512]{2,1,0:T(8,128)} %param.36) | copy-start | bytes 786436
  11.4 155.8 %all-gather.24.cloned.1.call-start = ((), (), s32[]{:S(2)}) async-start(), calls=%async_computation.24 | async-start | bytes 1769472 | tf_op jit(solution)/shard_map/all_gather | solution.py:532
  11.9 155.2 %all-gather.26.cloned.1.call-start = ((), (), s32[]{:S(2)}) async-start(), calls=%async_computation.25 | async-start | bytes 2359296 | tf_op jit(solution)/shard_map/all_gather | solution.py:534
  12.5 176.8 %all-gather.28.cloned.1.call-start = ((), (), s32[]{:S(2)}) async-start(), calls=%async_computation.26 | async-start | bytes 2359296 | tf_op jit(solution)/shard_map/all_gather | solution.py:535
  13.0 31.1 %copy-start.31 = (bf16[1024,128]{1,0:T(8,128)(2,1)}, bf16[1024,128]{1,0:T(8,128)(2,1)S(1)}, u32[]{:S(2)}) copy-start(bf16[1024,128]{1,0:T(8,128)(2,1)S(1)} %maximum_maximum_fusion.refs_2_.refs_19_) | copy-start | bytes 786436
  13.0 33.6 %collective-permute-start = (bf16[1024,128]{1,0:T(8,128)(2,1)S(1)}, bf16[1024,128]{1,0:T(8,128)(2,1)S(1)}, u32[]{:S(2)}, u32[]{:S(2)}) collective-permute-start(bf16[1024,128]{1,0:T(8,128)(2,1)S(1)} %maximum_maximum_fusion.refs_2_.refs_19_), channel_id=1, source_target_pairs={{0,8},{8,16},{16,24},{1,9},{9,17},{17,25},{2,10},{10,18},{18,26},{... | collective-permute-start | bytes 786440 | tf_op jit(solution)/shard_map/ppermute | solution.py:50
  18.0 215.4 %all-gather.16.cloned.1.call-start = ((), (), s32[]{:S(2)}) async-start(), calls=%async_computation.10 | async-start | bytes 1179648 | tf_op jit(solution)/shard_map/all_gather | solution.py:538
  28.2 15.9 %copy-start.26 = (bf16[512,128]{1,0:T(8,128)(2,1)}, bf16[512,128]{1,0:T(8,128)(2,1)S(1)}, u32[]{:S(2)}) copy-start(bf16[512,128]{1,0:T(8,128)(2,1)S(1)} %all_gather.30.refs_4_) | copy-start | bytes 393220
  32.2 13.0 %copy-start.11 = (bf16[2,2,512,512]{3,2,1,0:T(8,128)(2,1)S(1)}, bf16[2,2,512,512]{3,2,1,0:T(8,128)(2,1)}, u32[]{:S(2)}) copy-start(bf16[2,2,512,512]{3,2,1,0:T(8,128)(2,1)} %param.32) | copy-start | bytes 6291460
  46.6 54.2 %copy-start.54 = (bf16[1024,128]{1,0:T(8,128)(2,1)}, bf16[1024,128]{1,0:T(8,128)(2,1)S(1)}, u32[]{:S(2)}) copy-start(bf16[1024,128]{1,0:T(8,128)(2,1)S(1)} %collective-permute-done.refs_3_.refs_20_) | copy-start | bytes 786436
  100.8 52.4 %copy-start.10 = (f32[64,1024]{1,0:T(8,128)S(1)}, f32[64,1024]{1,0:T(8,128)}, u32[]{:S(2)}) copy-start(f32[64,1024]{1,0:T(8,128)} %param.39) | copy-start | bytes 786436
  100.8 53.4 %copy-start.50 = (s32[2,512]{1,0:T(2,128)S(1)}, s32[2,512]{1,0:T(2,128)}, u32[]{:S(2)}) copy-start(s32[2,512]{1,0:T(2,128)} %param.30) | copy-start | bytes 12292
  100.8 54.4 %copy-start.52 = (s32[2]{0:T(128)S(1)}, s32[2]{0:T(128)}, u32[]{:S(2)}) copy-start(s32[2]{0:T(128)} %param.31) | copy-start | bytes 28
  100.8 55.5 %copy-start.32 = (bf16[1,64,512]{2,1,0:T(8,128)(2,1)S(1)}, bf16[1,64,512]{2,1,0:T(8,128)(2,1)}, u32[]{:S(2)}) copy-start(bf16[1,64,512]{2,1,0:T(8,128)(2,1)} %get-tuple-element.290) | copy-start | bytes 196612
  148.9 40.5 %collective-permute-start.1 = (bf16[1024,512]{1,0:T(8,128)(2,1)}, bf16[1024,512]{1,0:T(8,128)(2,1)}, u32[]{:S(2)}, u32[]{:S(2)}) collective-permute-start(bf16[1024,512]{1,0:T(8,128)(2,1)} %get-tuple-element.77.refs_3_.refs_2_), channel_id=1, source_target_pairs={{0,8},{8,16},{16,24},{1,9},{9,17},{17,25},{2,10},{10,18},{18,26},{... | collective-permute-start | bytes 3145736 | tf_op jit(solution)/shard_map/ppermute | solution.py:50
  153.9 244.5 %reduce-scatter.19.cloned.1.call-start = ((), (), s32[]{:S(2)}) async-start(), calls=%async_computation.15 | async-start | bytes 589824 | tf_op jit(solution)/shard_map/reduce_scatter | solution.py:653
  301.7 27.5 %collective-permute-start.2 = (bf16[1024,512]{1,0:T(8,128)(2,1)}, bf16[1024,512]{1,0:T(8,128)(2,1)}, u32[]{:S(2)}, u32[]{:S(2)}) collective-permute-start(bf16[1024,512]{1,0:T(8,128)(2,1)} %get-tuple-element.108), channel_id=1, source_target_pairs={{8,0},{16,8},{24,16},{9,1},{17,9},{25,17},{10,2},{18,10},{26,18},{... | collective-permute-start | bytes 3145736 | tf_op jit(solution)/shard_map/ppermute | solution.py:50
  303.0 95.4 %reduce-scatter.29.cloned.1.call-start = ((), (), s32[]{:S(2)}) async-start(), calls=%async_computation.20 | async-start | bytes 1179648 | tf_op jit(solution)/shard_map/reduce_scatter | solution.py:653
  303.8 120.7 %reduce-scatter.17.cloned.1.call-start = ((), (), s32[]{:S(2)}) async-start(), calls=%async_computation.14 | async-start | bytes 589824 | tf_op jit(solution)/shard_map/reduce_scatter | solution.py:653
  391.1 75.2 %reduce-scatter.15.cloned.1.call-start = ((), (), s32[]{:S(2)}) async-start(), calls=%async_computation.13 | async-start | bytes 1769472 | tf_op jit(solution)/shard_map/reduce_scatter | solution.py:653
  391.9 118.8 %reduce-scatter.23.cloned.1.call-start = ((), (), s32[]{:S(2)}) async-start(), calls=%async_computation.17 | async-start | bytes 2359296 | tf_op jit(solution)/shard_map/reduce_scatter | solution.py:653
  392.4 163.1 %reduce-scatter.27.cloned.1.call-start = ((), (), s32[]{:S(2)}) async-start(), calls=%async_computation.19 | async-start | bytes 2359296 | tf_op jit(solution)/shard_map/reduce_scatter | solution.py:653
  393.2 204.0 %reduce-scatter.13.cloned.1.call-start = ((), (), s32[]{:S(2)}) async-start(), calls=%async_computation.12 | async-start | bytes 1769472 | tf_op jit(solution)/shard_map/reduce_scatter | solution.py:653
  393.8 247.8 %reduce-scatter.21.cloned.1.call-start = ((), (), s32[]{:S(2)}) async-start(), calls=%async_computation.16 | async-start | bytes 2359296 | tf_op jit(solution)/shard_map/reduce_scatter | solution.py:653
  394.4 292.0 %reduce-scatter.25.cloned.1.call-start = ((), (), s32[]{:S(2)}) async-start(), calls=%async_computation.18 | async-start | bytes 2359296 | tf_op jit(solution)/shard_map/reduce_scatter | solution.py:653
  394.4 292.7 %copy-start.45 = (f32[11,64]{1,0:T(8,128)S(1)}, f32[11,64]{1,0:T(8,128)}, u32[]{:S(2)}) copy-start(f32[11,64]{1,0:T(8,128)} %param.48) | copy-start | bytes 8452
  394.4 293.4 %copy-start.46 = (f32[11,64]{1,0:T(8,128)S(1)}, f32[11,64]{1,0:T(8,128)}, u32[]{:S(2)}) copy-start(f32[11,64]{1,0:T(8,128)} %param.56) | copy-start | bytes 8452
  394.4 295.3 %copy-start.48 = (f32[8,128]{1,0:T(8,128)S(1)}, f32[8,128]{1,0:T(8,128)}, u32[]{:S(2)}) copy-start(f32[8,128]{1,0:T(8,128)} %get-tuple-element.123) | copy-start | bytes 12292
  394.4 295.4 %copy-start.49 = (f32[8,128]{1,0:T(8,128)S(1)}, f32[8,128]{1,0:T(8,128)}, u32[]{:S(2)}) copy-start(f32[8,128]{1,0:T(8,128)} %get-tuple-element.122) | copy-start | bytes 12292
  394.9 334.9 %reduce-scatter.11.cloned.1.call-start = ((), (), s32[]{:S(2)}) async-start(), calls=%async_computation.11 | async-start | bytes 147456 | tf_op jit(solution)/shard_map/reduce_scatter | solution.py:653
  397.5 429.9 %copy-start.42 = (f32[80,64]{0,1:T(8,128)S(1)}, f32[80,64]{0,1:T(8,128)}, u32[]{:S(2)}) copy-start(f32[80,64]{0,1:T(8,128)} %param.42) | copy-start | bytes 61444
  397.5 429.9 %copy-start.43 = (f32[80,64]{0,1:T(8,128)S(1)}, f32[80,64]{0,1:T(8,128)}, u32[]{:S(2)}) copy-start(f32[80,64]{0,1:T(8,128)} %param.50) | copy-start | bytes 61444
  398.3 430.4 %copy-start.4 = (f32[2,64,1536]{2,1,0:T(8,128)S(1)}, f32[2,64,1536]{2,1,0:T(8,128)}, u32[]{:S(2)}) copy-start(f32[2,64,1536]{2,1,0:T(8,128)} %param.35) | copy-start | bytes 2359300
  398.3 430.4 %copy-start.24 = (f32[2,64,1536]{2,1,0:T(8,128)S(1)}, f32[2,64,1536]{2,1,0:T(8,128)}, u32[]{:S(2)}) copy-start(f32[2,64,1536]{2,1,0:T(8,128)} %param.43) | copy-start | bytes 2359300
  398.3 405.1 %all-reduce.10.cloned.1.call-start = ((), (), s32[]{:S(2)}) async-start(), calls=%async_computation.27 | async-start | bytes 3407872 | tf_op jit(solution)/shard_map/psum | solution.py:659
  729.8 102.3 %copy-start.51 = (f32[2,8]{1,0:T(2,128)}, f32[2,8]{1,0:T(2,128)S(1)}, u32[]{:S(2)}) copy-start(f32[2,8]{1,0:T(2,128)S(1)} %get-tuple-element.249) | copy-start | bytes 196
  828.7 4.9 copy-start.1
  828.8 4.9 copy-start.12
  846.7 27.9 %copy-start.28 = (f32[80,64]{0,1:T(8,128)S(1)}, f32[80,64]{0,1:T(8,128)}, u32[]{:S(2)}) copy-start(f32[80,64]{0,1:T(8,128)} %param.34) | copy-start | bytes 61444
  873.3 5.6 copy-start.20
  873.3 5.6 copy-start.21
  (29 other events, 90.0 us)
Sparse Core Ops, SparseCore 0:
  10.5 28.8 all-gather.17
  41.9 28.4 all-gather.19
  72.9 27.8 all-gather.21
  103.1 25.7 all-gather.23
  131.2 27.8 all-gather.25
  161.4 27.8 all-gather.27
  191.8 23.5 all-gather.15
  303.2 36.2 reduce-scatter.18
  342.9 36.0 reduce-scatter.28
  391.3 33.1 reduce-scatter.16
  427.8 38.4 reduce-scatter.14
  469.5 41.1 reduce-scatter.22
  514.3 41.2 reduce-scatter.26
  558.7 38.4 reduce-scatter.12
  600.4 41.1 reduce-scatter.20
  645.1 41.2 reduce-scatter.24
  689.7 33.4 reduce-scatter.10
  726.5 76.9 all-reduce.9

commit v2 on v1

--- a/solution.py
+++ b/solution.py
@@ -44,6 +44,146 @@
     return lax.dot_general(left, right, dims, preferred_element_type=f32)
 
 
+MESH = pl.DeviceIdType.MESH
+
+
+class Place:
+    def __init__(self, streams, blocks):
+        self.chips = streams // 2
+        self.blocks = blocks
+        index = lax.axis_index("stream")
+        self.chip = index // 2
+        self.core = index % 2
+        self.block = lax.axis_index("seq")
+        self.sibling = {"stream": 2 * self.chip + 1 - self.core}
+
+    def other(self, distance):
+        return (self.chip + distance) % self.chips
+
+    def mate(self, distance):
+        return {"stream": 2 * self.other(distance) + self.core}
+
+    def greet(self, line=False):
+        barrier = pltpu.get_barrier_semaphore()
+
+        def hello(device):
+            pl.semaphore_signal(barrier, inc=1, device_id=device, device_id_type=MESH)
+
+        hello(self.sibling)
+        for distance in range(1, self.chips):
+            hello(self.mate(distance))
+        if line:
+
+            @pl.when(self.block > 0)
+            def _():
+                hello({"seq": self.block - 1})
+
+            pl.semaphore_wait(barrier, self.chips + jnp.where(self.block < self.blocks - 1, 1, 0))
+        else:
+            pl.semaphore_wait(barrier, self.chips)
+
+
+class Gather:
+    def __init__(self, place, refs, sems, first):
+        self.place, self.refs, self.sems, self.first = place, refs, sems, first
+
+    def far(self, index, distance):
+        place, ref = self.place, self.refs[index]
+        out_sem, in_sem = self.sems[0], self.sems[1]
+        return pltpu.make_async_remote_copy(
+            src_ref=ref.at[place.chip, place.core],
+            dst_ref=ref.at[place.chip, place.core],
+            send_sem=out_sem.at[self.first + index, distance],
+            recv_sem=in_sem.at[self.first + index, distance],
+            device_id=place.mate(distance),
+            device_id_type=MESH,
+        )
+
+    def near(self, index, core):
+        place, ref = self.place, self.refs[index]
+        out_sem, in_sem = self.sems[0], self.sems[1]
+        return pltpu.make_async_remote_copy(
+            src_ref=ref.at[:, core],
+            dst_ref=ref.at[:, core],
+            send_sem=out_sem.at[self.first + index, 0],
+            recv_sem=in_sem.at[self.first + index, 0],
+            device_id=place.sibling,
+            device_id_type=MESH,
+        )
+
+    def push(self):
+        for index in range(len(self.refs)):
+            for distance in range(1, self.place.chips):
+                self.far(index, distance).start()
+
+    def relay(self):
+        place = self.place
+        for index in range(len(self.refs)):
+            ref = self.refs[index]
+            for distance in range(1, place.chips):
+                source = place.other(place.chips - distance)
+                pltpu.make_async_remote_copy(
+                    src_ref=ref.at[source, place.core],
+                    dst_ref=ref.at[source, place.core],
+                    send_sem=self.sems[0].at[self.first + index, distance],
+                    recv_sem=self.sems[1].at[self.first + index, distance],
+                    device_id=place.mate(distance),
+                    device_id_type=MESH,
+                ).wait_recv()
+            self.near(index, place.core).start()
+
+    def finish(self):
+        place = self.place
+        for index in range(len(self.refs)):
+            self.near(index, 1 - place.core).wait_recv()
+            self.near(index, place.core).wait_send()
+            for distance in range(1, place.chips):
+                self.far(index, distance).wait_send()
+
+
+class Ahead:
+    def __init__(self, place, step, src, dst, sems):
+        self.place, self.step, self.src, self.dst, self.sems = place, step, src, dst, sems
+        self.sends = place.block < place.blocks - 1 if step > 0 else place.block > 0
+        self.receives = place.block > 0 if step > 0 else place.block < place.blocks - 1
+
+    def copy(self, slot, rows):
+        return pltpu.make_async_remote_copy(
+            src_ref=self.src.at[rows],
+            dst_ref=self.dst.at[rows],
+            send_sem=self.sems[0].at[slot],
+            recv_sem=self.sems[1].at[slot],
+            device_id={"seq": self.place.block + self.step},
+            device_id_type=MESH,
+        )
+
+    def start(self, slot, rows):
+        @pl.when(self.sends)
+        def _():
+            self.copy(slot, rows).start()
+
+    def arrived(self, slot, rows):
+        @pl.when(self.receives)
+        def _():
+            self.copy(slot, rows).wait_recv()
+
+    def sent(self, slot, rows):
+        @pl.when(self.sends)
+        def _():
+            self.copy(slot, rows).wait_send()
+
+
+def flat(ref, cols=slice(None)):
+    value = ref[:, :, :, cols]
+    return value.reshape((-1, value.shape[-1]))
+
+
+def flat_rows(ref, part, parts):
+    chips = ref.shape[0] // parts
+    value = ref[pl.ds(part * chips, chips)]
+    return value.reshape((-1, value.shape[-1]))
+
+
 def from_behind(block, axis, distance):
     devices = range(lax.axis_size(axis))
     route = [(i - distance, i) for i in devices if i - distance in devices]
@@ -88,7 +228,7 @@
     return (left, right)
 
 
-def attend(streams, span, heads, q_ref, k_ref, v_ref, kf_ref, qf_ref, o_ref, lse_ref):
+def attend(streams, span, heads, q_ref, k_ref, v_ref, kf_ref, qf_ref, o_ref, lse_ref, between):
     pairs = heads // 2
     step = span // 2
     masks = half_masks()
@@ -135,20 +275,65 @@
             one(stream, pair)
             return carry
 
-        return lax.fori_loop(0, pairs, inner, carry)
+        carry = lax.fori_loop(0, pairs, inner, carry)
+        between(stream)
+        return carry
 
     lax.fori_loop(0, streams, over, 0)
 
 
-def forward_kernel(layer, streams, span, heads, *refs):
-    n_in = 12
+def forward_kernel(layer, sizes, *refs):
+    (stream_devices, block_devices, streams, span, heads, features, nvec) = sizes
+    place = Place(stream_devices, block_devices)
+    chip, core = place.chip, place.core
     if layer == 0:
-        (first_ref, rows_ref, frames_ref, halo_ref, small_ref, mem_ref, kf_ref, qf_ref, wp, wo, wu, wd) = refs[:n_in]
-        (r_ref, low_ref, pr_ref, a_ref, ap_ref, q_ref, k_ref, v_ref, o_ref, lse_ref, r1_ref, a2_ref, u_ref, gp_ref, out_ref, next_ref) = refs[n_in:]
+        (first_ref, small_own, frames_ref, mem_ref, kf_ref, qf_ref, pw, ow, uw, dw) = refs[:10]
+        (rows_ref, r_ref, low_ref, pr_ref, a_ref, ap_ref, q_ref, k_ref, v_ref, o_ref, lse_ref, r1_ref, a2_ref, u_ref, gp_ref, out_ref) = refs[10:26]
+        (next_ref, behind_ref, halo_ref, small, wp, wo, wu, wd, wp_next, wo_next) = refs[26:36]
+        (out_sem, in_sem, frame_sem, next_out, next_in) = refs[36:]
+        sems = (out_sem, in_sem)
+        early = Gather(place, [small, wp], sems, 0)
+        middle = Gather(place, [wo, wu, wd], sems, 2)
+        late = Gather(place, [wp_next, wo_next], sems, 5)
+        frames_ahead = Ahead(place, 1, frames_ref, halo_ref, (frame_sem.at[0], frame_sem.at[1]))
+        next_ahead = Ahead(place, 1, next_ref, behind_ref, (next_out, next_in))
+        every = pl.ds(0, streams * span)
+
+        @pl.when(place.block == 0)
+        def _():
+            halo_ref[...] = jnp.zeros_like(halo_ref)
+            behind_ref[...] = jnp.zeros_like(behind_ref)
+
+        small[chip, core] = small_own[...]
+        wp[chip, core] = pw[0].astype(bf16)
+        place.greet(line=True)
+        early.push()
+        frames_ahead.start(0, every)
+        wo[chip, core] = ow[0].astype(bf16)
+        wu[chip, core] = uw[0].astype(bf16)
+        wd[chip, core] = dw[0].astype(bf16)
+        wp_next[chip, core] = pw[1].astype(bf16)
+        wo_next[chip, core] = ow[1].astype(bf16)
+        early.relay()
+        middle.push()
+        early.finish()
+        turned = flat(small).astype(f32).T
+        rows_ref[...] = jnp.zeros_like(rows_ref)
+        rows_ref[:nvec, :] = turned[features : features + nvec]
+        frames_ahead.arrived(0, every)
+        halfway = middle
     else:
-        (first_ref, rows_ref, r_ref, a_ref, halo_ref, mem_ref, kf_ref, qf_ref, wp, wo, wu, wd) = refs[:n_in]
-        (low_ref, ap_ref, q_ref, k_ref, v_ref, o_ref, lse_ref, r1_ref, a2_ref, u_ref, gp_ref, out_ref) = refs[n_in:]
-    width = wp.shape[0]
+        (first_ref, rows_ref, r_ref, a_ref, halo_ref, mem_ref, kf_ref, qf_ref, wp, wo, uw, dw, hw) = refs[:13]
+        (low_ref, ap_ref, q_ref, k_ref, v_ref, o_ref, lse_ref, r1_ref, a2_ref, u_ref, gp_ref, out_ref) = refs[13:25]
+        (wu, wd, wh) = refs[25:28]
+        (out_sem, in_sem) = refs[28:]
+        halfway = Gather(place, [wu, wd, wh], (out_sem, in_sem), 0)
+        wu[chip, core] = uw[1].astype(bf16)
+        wd[chip, core] = dw[1].astype(bf16)
+        wh[chip, core] = hw[...].astype(bf16)
+        place.greet()
+        halfway.push()
+    width = a_ref.shape[1]
     first = first_ref[0] > 0
     row = 3 + 4 * layer
     g1, b1, g2, b2 = (rows_ref[row + i : row + i + 1, :] for i in range(4))
@@ -161,12 +346,12 @@
             behind = pl.ds(pl.multiple_of(stream * 2 * span + part * step, step), step)
             here = pl.ds(pl.multiple_of(stream * 2 * span + span + part * step, step), step)
             if layer == 0:
-                r = mm(frames_ref[at, :], small_ref[...], NT)
+                r = mm(frames_ref[at, :], flat(small), NT)
                 r_ref[at, :] = r
                 low_ref[at, :] = r.astype(bf16)
                 a = (normalize(r)[0] * g1 + b1).astype(bf16)
                 a_ref[at, :] = a
-                before = mm(halo_ref[at, :], small_ref[...], NT)
+                before = mm(halo_ref[at, :], flat(small), NT)
                 before = jnp.where(first, mem_ref[at, :].astype(f32), before)
                 pr_ref[at, :] = before
                 ap = (normalize(before)[0] * g1 + b1).astype(bf16)
@@ -176,37 +361,61 @@
                 ap = (normalize(mem_ref[at, :].astype(f32))[0] * g1 + b1).astype(bf16)
                 ap = jnp.where(first, ap.astype(f32), halo_ref[at, :].astype(f32)).astype(bf16)
             ap_ref[at, :] = ap
-            q_ref[at, :] = (mm(a, wp[:, :width]) * 0.125).astype(bf16)
-            k_ref[here, :] = mm(a, wp[:, width : 2 * width]).astype(bf16)
-            v_ref[here, :] = mm(a, wp[:, 2 * width :]).astype(bf16)
-            k_ref[behind, :] = mm(ap, wp[:, width : 2 * width]).astype(bf16)
-            v_ref[behind, :] = mm(ap, wp[:, 2 * width :]).astype(bf16)
+            wq, wk, wv = (flat(wp, slice(i * width, (i + 1) * width)) for i in range(3))
+            q_ref[at, :] = (mm(a, wq) * 0.125).astype(bf16)
+            k_ref[here, :] = mm(a, wk).astype(bf16)
+            v_ref[here, :] = mm(a, wv).astype(bf16)
+            k_ref[behind, :] = mm(ap, wk).astype(bf16)
+            v_ref[behind, :] = mm(ap, wv).astype(bf16)
         return carry
 
     for_streams(project, 0)
-    attend(streams, span, heads, q_ref, k_ref, v_ref, kf_ref, qf_ref, o_ref, lse_ref)
+
+    def between(stream):
+        @pl.when(stream == 0)
+        def _():
+            halfway.relay()
+            if layer == 0:
+                late.push()
+
+    attend(streams, span, heads, q_ref, k_ref, v_ref, kf_ref, qf_ref, o_ref, lse_ref, between)
+    halfway.finish()
 
     def feed(stream, carry):
         at = tile(stream, span)
-        after = r_ref[at, :] + mm(o_ref[at, :], wo[...])
+        after = r_ref[at, :] + mm(o_ref[at, :], flat(wo))
         r1_ref[at, :] = after
         a2 = (normalize(after)[0] * g2 + b2).astype(bf16)
         a2_ref[at, :] = a2
         total = after
-        for part in range(wu.shape[1] // 512):
+        parts = wu.shape[3] // 512
+        for part in range(parts):
             cols = slice(part * 512, (part + 1) * 512)
-            active, slope = gelu_pair(mm(a2, wu[:, cols]))
+            active, slope = gelu_pair(mm(a2, flat(wu, cols)))
             active = active.astype(bf16)
             u_ref[at, cols] = active
             gp_ref[at, cols] = slope.astype(bf16)
-            total = total + mm(active, wd[cols, :])
+            total = total + mm(active, flat_rows(wd, part, parts))
         out_ref[at, :] = total
         if layer == 0:
             g, b = rows_ref[row + 4 : row + 5, :], rows_ref[row + 5 : row + 6, :]
             next_ref[at, :] = (normalize(total)[0] * g + b).astype(bf16)
+            next_ahead.start(stream, at)
+
+            @pl.when(stream == 0)
+            def _():
+                late.relay()
+
         return carry
 
     for_streams(feed, 0)
+    if layer == 0:
+        late.finish()
+        frames_ahead.sent(0, every)
+        for stream in range(streams):
+            at = tile(stream, span)
+            next_ahead.sent(stream, at)
+            next_ahead.arrived(stream, at)
 
 
 def head_kernel(rows_ref, r_ref, wh, target_ref, share_ref, dwh_ref, dr_ref, gr_ref, loss_ref, acc):
@@ -220,7 +429,7 @@
         at = tile(index, step)
         standard, scale = normalize(r_ref[at, :])
         f = (standard * gain + bias).astype(bf16)
-        z = mm(f, wh[...])
+        z = mm(f, flat(wh))
         share = share_ref[at, :]
         peak = jnp.max(z, axis=-1, keepdims=True)
         raised = jnp.exp(z - peak)
@@ -232,7 +441,7 @@
         soft = raised * (1.0 / total)
         dz = (share * jnp.where(hit, soft - 1.0, soft)).astype(bf16)
         acc[...] += mm(f, dz, TN)
-        df = mm(dz, wh[...], NT)
+        df = mm(dz, flat(wh), NT)
         gr_ref[0:1, :] += jnp.sum(df * standard, axis=0, keepdims=True)
         gr_ref[1:2, :] += jnp.sum(df, axis=0, keepdims=True)
         dr_ref[at, :] = norm_back(df, standard, scale, gain)
@@ -321,7 +530,7 @@
         (dwp, dwo, dwu, dwd, gr_ref, gs_ref, dr1_out, da_out, dap_out) = rest[2:11]
         scratch = rest[11:]
     (dr_ref, da_ref, do_ref, dq_ref, dk_ref, dv_ref, dk_acc, dv_acc, tr_ref) = scratch
-    width = wp.shape[0]
+    width = a_ref.shape[1]
     count = streams * span
     first = first_ref[0] > 0
     row = 3 + 4 * layer
@@ -355,16 +564,18 @@
     da_ref[...] = jnp.zeros_like(da_ref)
     tr_ref[...] = a2_ref[...].T
 
+    parts = wu.shape[3] // 512
+
     def feed(part, carry):
         cols = tile(part, 512)
         dy = dr_ref[...].astype(bf16)
-        dh = (mm(dy, wd[cols, :], NT) * gp_ref[:, cols].astype(f32)).astype(bf16)
+        dh = (mm(dy, flat_rows(wd, part, parts), NT) * gp_ref[:, cols].astype(f32)).astype(bf16)
         dwd[cols, :] = mm(u_ref[:, cols], dy, TN).astype(bf16)
         dwu[:, cols] = mm(tr_ref[...], dh).astype(bf16)
-        da_ref[...] += mm(dh, wu[:, cols], NT)
+        da_ref[...] += mm(dh, flat(wu, cols), NT)
         return carry
 
-    lax.fori_loop(0, wu.shape[1] // 512, feed, 0)
+    lax.fori_loop(0, parts, feed, 0)
 
     def middle(index, carry):
         at = tile(index, step)
@@ -374,7 +585,7 @@
         gr_ref[3:4, :] += jnp.sum(da, axis=0, keepdims=True)
         dr = dr_ref[at, :] + norm_back(da, standard, scale, g2)
         dr_ref[at, :] = dr
-        do_ref[at, :] = mm(dr.astype(bf16), wo[...], NT).astype(bf16)
+        do_ref[at, :] = mm(dr.astype(bf16), flat(wo), NT).astype(bf16)
         return carry
 
     lax.fori_loop(0, tiles, middle, 0)
@@ -407,7 +618,7 @@
             at = pl.ds(pl.multiple_of(stream * span + part * step, step), step)
             behind = pl.ds(pl.multiple_of(stream * 2 * span + part * step, step), step)
             here = pl.ds(pl.multiple_of(stream * 2 * span + span + part * step, step), step)
-            wq, wk, wv = (wp[:, i * width : (i + 1) * width] for i in range(3))
+            wq, wk, wv = (flat(wp, slice(i * width, (i + 1) * width)) for i in range(3))
             da = mm(dq_ref[at, :], wq, NT) + mm(dk_ref[here, :], wk, NT) + mm(dv_ref[here, :], wv, NT)
             dap = mm(dk_ref[behind, :], wk, NT) + mm(dv_ref[behind, :], wv, NT)
             if layer == 0:
@@ -438,7 +649,7 @@
     return pl.BlockSpec(memory_space=space)
 
 
-def call(kernel, name, args, outs, scratch=(), smem=1, flops=0):
+def call(kernel, name, args, outs, scratch=(), smem=1, flops=0, sems=(), collective=None):
     specs = [whole(pltpu.SMEM)] * smem + [whole()] * (len(args) - smem)
     return pl.pallas_call(
         kernel,
@@ -446,8 +657,10 @@
         out_shape=[jax.ShapeDtypeStruct(*out) for out in outs],
         in_specs=specs,
         out_specs=[whole()] * len(outs),
-        scratch_shapes=[pltpu.VMEM(*item) for item in scratch],
-        compiler_params=pltpu.CompilerParams(vmem_limit_bytes=VMEM_LIMIT),
+        scratch_shapes=[pltpu.VMEM(*item) for item in scratch] + list(sems),
+        compiler_params=pltpu.CompilerParams(
+            vmem_limit_bytes=VMEM_LIMIT, collective_id=collective, has_side_effects=collective is not None
+        ),
         cost_estimate=pl.CostEstimate(flops=flops, bytes_accessed=20000000, transcendentals=0),
     )(*args)
 
@@ -523,26 +736,10 @@
     small_own = jnp.concatenate(
         [input_weight.T, vectors.T, jnp.zeros((input_weight.shape[1], 128 - features - nvec), f32)], axis=1
     ).astype(bf16)
-    gather = functools.partial(lax.all_gather, axis_name="stream", tiled=True)
-    small = gather(small_own, axis=0)
-    weights_low = []
-    for layer in range(layers):
-        weights_low.append(
-            (
-                gather(project_weight[layer].astype(bf16), axis=0),
-                gather(output_weight[layer].astype(bf16), axis=0),
-                gather(up_weight[layer].astype(bf16), axis=0),
-                gather(down_weight[layer].astype(bf16), axis=0),
-            )
-        )
-    head_low = gather(head_weight.astype(bf16), axis=0)
-    rows = jnp.pad(small[:, features : features + nvec].astype(f32).T, ((0, 16 - nvec), (0, 0)))
-
     frames_flat = frames.reshape((count, features))
     frames_flat = jnp.concatenate(
         [frames_flat, jnp.ones((count, 1), bf16), jnp.zeros((count, 127 - features), bf16)], axis=1
     )
-    frames_behind = from_behind(frames_flat, "seq", 1)
     memory_flat = memory.reshape((layers, count, width))
 
     key_pos = jnp.arange(2 * span)
@@ -572,27 +769,48 @@
     saved_outs = [low, low, joined, joined, low, lse, full, low, wide, wide, full]
     cost = 2 * count * (5 * width * width + width * width + 2 * width * hidden) + 4 * count * 2 * span * width
 
+    devices = lax.axis_size("stream")
+    chips = devices // 2
+    sizes = (devices, lax.axis_size("seq"), streams, span, heads, features, nvec)
+
+    def gathered(rows_all, cols):
+        return ((chips, 2, rows_all // devices, cols), bf16)
+
+    project_shape = gathered(width, 3 * width)
+    output_shape = gathered(width, width)
+    up_shape = gathered(width, hidden)
+    down_shape = gathered(hidden, width)
+    dma = pltpu.SemaphoreType.DMA
     made = call(
-        functools.partial(forward_kernel, 0, streams, span, heads),
+        functools.partial(forward_kernel, 0, sizes),
         "forward_zero",
-        (first_flag, rows, frames_flat, frames_behind, small, memory_flat[0], key_marks, query_marks[0]) + weights_low[0],
-        [full, low, full, low] + saved_outs + [low],
+        (first_flag, small_own, frames_flat, memory_flat[0], key_marks, query_marks[0], project_weight, output_weight, up_weight, down_weight),
+        [((16, width), f32), full, low, full, low]
+        + saved_outs
+        + [low, low, ((count, 128), bf16), gathered(width, 128), project_shape, output_shape, up_shape, down_shape, project_shape, output_shape],
+        sems=(dma((7, chips)), dma((7, chips)), dma((2, 1)), dma((streams,)), dma((streams,))),
         flops=cost,
-    )
-    r_zero, low_zero, pr_zero, a_zero = made[:4]
-    saved_zero = made[4:14]
-    r_one, a_one = made[14:16]
-    a_behind = from_behind(a_one, "seq", 1)
+        collective=0,
+    )
+    rows, r_zero, low_zero, pr_zero, a_zero = made[:5]
+    saved_zero = made[5:15]
+    r_one, a_one, a_behind, frames_behind = made[15:19]
+    weights_zero = made[20:24]
+    project_one, output_one = made[24:]
     made = call(
-        functools.partial(forward_kernel, 1, streams, span, heads),
+        functools.partial(forward_kernel, 1, sizes),
         "forward_one",
-        (first_flag, rows, r_one, a_one, a_behind, memory_flat[1], key_marks, query_marks[1]) + weights_low[1],
-        [low] + saved_outs,
+        (first_flag, rows, r_one, a_one, a_behind, memory_flat[1], key_marks, query_marks[1], project_one, output_one, up_weight, down_weight, head_weight),
+        [low] + saved_outs + [up_shape, down_shape, gathered(width, codes)],
+        sems=(dma((3, chips)), dma((3, chips))),
         flops=cost,
+        collective=1,
     )
     low_one = made[0]
     saved_one = made[1:11]
     r_two = made[11]
+    up_one, down_one, head_low = made[12:]
+    weights_low = (weights_zero, (project_one, output_one, up_one, down_one))
 
     position = seq_index * span + jnp.arange(span)
     share = jnp.where(

time: 896 us -> 846 us (0.944)
  waiting for transfers between devices: 449 us -> 371 us
  Pallas kernels: 222 us -> 290 us
  blocking collectives: 116 us -> 84.5 us
  starting transfers between devices: 11.5 us -> 1.97 us
    all_gather x7 -> x0, waiting for transfers between devices: 76.4 us -> none  [the longest x2 52.6 us: shards(): gather(down_weight[layer].astype(bf16), axis=0)]
    pallas_call x5, Pallas kernels: 222 us -> 290 us  [call(): pl.pallas_call(kernel, name=name, out_shape=[jax.ShapeDtypeStruct(*out) f...]
    all_gather x3 -> x0, blocking collectives: 31.6 us -> none  [the longest x2 22.4 us: shards(): gather(output_weight[layer].astype(bf16), axis=0)]
    ppermute x3 -> x1, starting transfers between devices: 10.6 us -> 1.29 us  [from_behind(): return lax.ppermute(block, axis, route)]
    ppermute x3 -> x1, waiting for transfers between devices: 25.4 us -> 24.7 us  [from_behind(): return lax.ppermute(block, axis, route)]
  transfers between devices with their start and end apart: 21 -> 12, of which waited for: 12 -> 9; matrix products, arithmetic and copies ran while one was open for 2% -> 1% of each run, Pallas kernels for 17% -> 7%
where the time goes in v2:
time: 846 us; the launch traced here: 835 us
  waiting for transfers between devices  371 us (44%)
  Pallas kernels  290 us (34%)
  blocking collectives  84.5 us (10%)
  other arithmetic  47.1 us (6%)
  local copies, waits for them, and re-layouts  20.9 us (2%)
  between operations  20.2 us (2%)
    pallas_call x5, Pallas kernels, call(): pl.pallas_call(kernel, name=name, out_shape=[jax.ShapeDtypeStruct(*out) f...  290 us
    reduce_scatter x10, waiting for transfers between devices, scatter(): return lax.psum_scatter(grad, 'stream', scatter_dimension=0, tiled=True)  289 us
    psum x1, waiting for transfers between devices, shards(): lax.psum((head_share, one_share, zero_share, small_share), 'seq')  53.1 us
    psum x1, blocking collectives, shards(): loss, grad_slopes = lax.psum((loss_term, grad_slopes), ('seq', 'stream'))  39.6 us
    ppermute x1, waiting for transfers between devices, from_behind(): return lax.ppermute(block, axis, route)  24.7 us
    psum x1, blocking collectives, shards(): lax.psum((head_share, one_share, zero_share, small_share), 'seq')  19.4 us
  transfers between devices with their start and end apart: 12, of which 9 were waited for; matrix products, arithmetic and copies ran while one was open for 1% of the time, Pallas kernels for 7%

profile of v2, /device:TPU:0, one launch (start us, length us, event | category | flops | bytes accessed | tf_op | source)
XLA Modules:
  0.0 835.4 jit_solution(3730690093352752110)
XLA Ops:
  7.3 1.4 multiply_reduce_fusion.15
  9.6 1.1 copy.125
  10.9 3.0 fusion.58
  15.8 1.0 copy.147
  16.9 1.0 copy.149
  17.9 1.1 pad_maximum_fusion.1.refs_4_.refs_6_.refs_13_
  21.3 96.1 %forward_zero.1 = (f32[16,512]{1,0:T(8,128)}, f32[1024,512]{1,0:T(8,128)}, bf16[1024,512]{1,0:T(8,128)(2,1)}, f32[1024,512]{1,0:T(8,128)}, bf16[1024,512]{1,0:T(...) custom-call(s32[1]{0:T(128)} %bitcast.refs_0_, ...), custom_call_target="tpu_custom_call" | custom-call | flops 9663676416 | bytes 20000000 | tf_op jit(solution)/shard_map/forward_zero/pallas_call | solution.py:654
  117.4 63.6 %forward_one.1 = (bf16[1024,512]{1,0:T(8,128)(2,1)}, bf16[1024,512]{1,0:T(8,128)(2,1)}, bf16[1024,512]{1,0:T(8,128)(2,1)}, bf16[2048,512]{1,0:T(8,128)(2,1)}, bf...) custom-call(s32[1]{0:T(128)} %bitcast.refs_0_, ...), custom_call_target="tpu_custom_call" | custom-call | flops 9663676416 | bytes 20000000 | tf_op jit(solution)/shard_map/forward_one/pallas_call | solution.py:654
  181.0 11.2 %head_loss.1 = (bf16[512,1024]{1,0:T(8,128)(2,1)}, f32[1024,512]{1,0:T(8,128)}, f32[8,512]{1,0:T(8,128)}, f32[8,128]{1,0:T(8,128)}) custom-call(f32[16,512]{1,0:T(8,128)} %get-tuple-element.88.refs_1_.rows_ref, f32[1024,512]{1,0:T(8,128)} %get-tuple-element.94.r_ref, bf16[4,2,64,1024]{3,2,1,0:T(8,128)(2,1)} %get-tuple-element.95.wh, s32[1024,1]{1,0:T(8,128)} %bitcast.83, ...), custom_call_target="tpu_custom_call" | custom-call | flops 3221225472 | bytes 20000000 | tf_op jit(solution)/shard_map/head_loss/pallas_call | solution.py:654
  192.2 57.0 %backward_one.1 = (bf16[512,1536]{1,0:T(8,128)(2,1)}, bf16[512,512]{1,0:T(8,128)(2,1)}, bf16[512,2048]{1,0:T(8,128)(2,1)}, bf16[2048,512]{1,0:T(8,128)(2,1)}, f3...) custom-call(s32[1]{0:T(128)} %bitcast.refs_0_, ...), custom_call_target="tpu_custom_call" | custom-call | flops 19327352832 | bytes 20000000 | tf_op jit(solution)/shard_map/backward_one/pallas_call | solution.py:654
  249.2 1.3 collective-permute-start
  251.4 24.7 %collective-permute-done.refs_25_ = bf16[1024,512]{1,0:T(8,128)(2,1)} collective-permute-done((bf16[1024,512]{1,0:T(8,128)(2,1)}, bf16[1024,512]{1,0:T(8,128)(2,1)}, u32[]{:S(2)}, u32[]{:S(2)}) %collective-permute-start) | collective-permute-done | bytes 1048608 | tf_op jit(solution)/shard_map/ppermute | solution.py:190
  276.0 61.7 %backward_zero.1 = (bf16[512,1536]{1,0:T(8,128)(2,1)}, bf16[512,512]{1,0:T(8,128)(2,1)}, bf16[512,2048]{1,0:T(8,128)(2,1)}, bf16[2048,512]{1,0:T(8,128)(2,1)}, f...) custom-call(s32[1]{0:T(128)} %bitcast.refs_0_, f32[16,512]{1,0:T(8,128)} %get-tuple-element.88.refs_1_.rows_ref, ...), custom_call_target="tpu_custom_call" | custom-call | flops 19327352832 | bytes 20000000 | tf_op jit(solution)/shard_map/backward_zero/pallas_call | solution.py:654
  345.4 26.6 %reduce-scatter.17.cloned.1.call-done = bf16[64,512]{1,0:T(8,128)(2,1)} async-done(((bf16[512,512]{1,0:T(8,128)(2,1)}), bf16[64,512]{1,0:T(8,128)(2,1)}) %reduce-scatter.17.cloned.1.call-update) | async-done | bytes 65552 | tf_op jit(solution)/shard_map/reduce_scatter | solution.py:871
  372.0 41.6 %reduce-scatter.15.cloned.1.call-done = bf16[64,1536]{1,0:T(8,128)(2,1)} async-done(((bf16[512,1536]{1,0:T(8,128)(2,1)}), bf16[64,1536]{1,0:T(8,128)(2,1)}) %reduce-scatter.15.cloned.1.call-update) | async-done | bytes 196624 | tf_op jit(solution)/shard_map/reduce_scatter | solution.py:871
  413.7 44.4 %reduce-scatter.23.cloned.1.call-done = bf16[64,2048]{1,0:T(8,128)(2,1)} async-done(((bf16[512,2048]{1,0:T(8,128)(2,1)}), bf16[64,2048]{1,0:T(8,128)(2,1)}) %reduce-scatter.23.cloned.1.call-update) | async-done | bytes 262160 | tf_op jit(solution)/shard_map/reduce_scatter | solution.py:871
  458.1 44.8 %reduce-scatter.27.cloned.1.call-done = bf16[256,512]{1,0:T(8,128)(2,1)} async-done(((bf16[2048,512]{1,0:T(8,128)(2,1)}), bf16[256,512]{1,0:T(8,128)(2,1)}) %reduce-scatter.27.cloned.1.call-update) | async-done | bytes 262160 | tf_op jit(solution)/shard_map/reduce_scatter | solution.py:871
  502.8 41.8 %reduce-scatter.13.cloned.1.call-done = bf16[64,1536]{1,0:T(8,128)(2,1)} async-done(((bf16[512,1536]{1,0:T(8,128)(2,1)}), bf16[64,1536]{1,0:T(8,128)(2,1)}) %reduce-scatter.13.cloned.1.call-update) | async-done | bytes 196624 | tf_op jit(solution)/shard_map/reduce_scatter | solution.py:871
  544.6 45.1 %reduce-scatter.21.cloned.1.call-done = bf16[64,2048]{1,0:T(8,128)(2,1)} async-done(((bf16[512,2048]{1,0:T(8,128)(2,1)}), bf16[64,2048]{1,0:T(8,128)(2,1)}) %reduce-scatter.21.cloned.1.call-update) | async-done | bytes 262160 | tf_op jit(solution)/shard_map/reduce_scatter | solution.py:871
  589.7 44.9 %reduce-scatter.25.cloned.1.call-done = bf16[256,512]{1,0:T(8,128)(2,1)} async-done(((bf16[2048,512]{1,0:T(8,128)(2,1)}), bf16[256,512]{1,0:T(8,128)(2,1)}) %reduce-scatter.25.cloned.1.call-update) | async-done | bytes 262160 | tf_op jit(solution)/shard_map/reduce_scatter | solution.py:871
  634.8 1.2 slice.83
  637.6 1.5 pad_maximum_fusion
  639.2 39.6 %all-reduce.4 = (f32[]{:T(128)}, f32[2,8]{1,0:T(2,128)S(1)}) all-reduce(f32[]{:T(128)} %bitcast.14, f32[2,8]{1,0:T(2,128)S(1)} %pad_maximum_fusion.7), channel_id=1, replica_groups=mesh['seq'=4,'stream'=8] {'seq','stream'}, use_global_device_ids=true, to_apply=%region_0.1 | all-reduce | flops 17 | bytes 136 | tf_op jit(solution)/shard_map/psum | solution.py:891
  678.8 19.4 %psum.106 = bf16[64,128]{1,0:T(8,128)(2,1)S(1)} all-reduce(bf16[64,128]{1,0:T(8,128)(2,1)} %reduce-scatter.11.cloned.1.call-done), channel_id=1, replica_groups=mesh['seq'=4,'stream'=8] {'seq'}, use_global_device_ids=true, to_apply=%region_2.3 | all-reduce | flops 8192 | bytes 32768 | tf_op jit(solution)/shard_map/psum | solution.py:877
  699.0 53.1 %all-reduce.9.cloned.1.call-done = (bf16[1,64,1536]{2,1,0:T(8,128)(2,1)}, bf16[1,64,1536]{2,1,0:T(8,128)(2,1)}, bf16[1,64,512]{2,1,0:T(8,128)(2,1)}, bf16[1,64,5...) async-done(((bf16[1,64,1536]{2,1,0:T(8,128)(2,1)}, ...) | async-done | bytes 1703952 | tf_op jit(solution)/shard_map/psum | solution.py:877
  752.1 1.6 fusion.17
  753.6 1.2 fusion.10
  754.9 1.0 fusion.16
  755.9 1.3 fusion.4
  757.1 1.3 fusion.5
  758.4 1.4 concatenate.44
  760.4 13.6 %psum.116 = f32[21]{0:T(128)S(1)} all-reduce(f32[21]{0:T(128)S(1)} %concatenate.44), channel_id=1, replica_groups=mesh['seq'=4,'stream'=8] {'stream'}, use_global_device_ids=true, to_apply=%region_28.29 | all-reduce | flops 21 | bytes 168 | tf_op jit(solution)/shard_map/psum | solution.py:892
  776.0 1.2 multiply_reduce_fusion.12
  777.4 3.3 multiply_reduce_fusion.5
  780.7 2.5 multiply_reduce_fusion.9
  783.3 2.4 multiply_reduce_fusion.3
  785.8 2.8 multiply_reduce_fusion.2
  788.6 1.7 multiply_reduce_fusion.8
  790.9 2.1 concatenate.46
  793.1 2.1 concatenate.45
  795.8 11.8 %all-reduce.5 = (f32[21]{0:T(128)S(1)}, f32[21]{0:T(128)S(1)}) all-reduce(f32[21]{0:T(128)S(1)} %concatenate.46, f32[21]{0:T(128)S(1)} %concatenate.45), channel_id=1, replica_groups=mesh['seq'=4,'stream'=8] {'stream'}, use_global_device_ids=true, to_apply=%region_47.48 | all-reduce | flops 42 | bytes 336 | tf_op jit(solution)/shard_map/psum | solution.py:929
  809.9 1.3 multiply_subtract_fusion.7
  816.7 1.4 pad_maximum_fusion.8
  818.0 1.4 multiply_subtract_fusion.6
  819.5 3.0 multiply_subtract_fusion.2
  822.5 0.9 multiply_subtract_fusion.4
  823.4 1.6 multiply_subtract_fusion.1
  824.9 1.5 multiply_subtract_fusion
  (190 shorter events, 24.8 us)
Async XLA Ops:
  7.2 338.2 %reduce-scatter.19.cloned.1.call-start = ((), (), s32[]{:S(2)}) async-start(), calls=%async_computation.14 | async-start | bytes 589824 | tf_op jit(solution)/shard_map/reduce_scatter | solution.py:871
  10.9 3.0 copy-start.47
  13.9 2.9 copy-start.46
  249.2 26.8 %collective-permute-start = (bf16[1024,512]{1,0:T(8,128)(2,1)}, bf16[1024,512]{1,0:T(8,128)(2,1)}, u32[]{:S(2)}, u32[]{:S(2)}) collective-permute-start(bf16[1024,512]{1,0:T(8,128)(2,1)} %get-tuple-element.132), channel_id=1, source_target_pairs={{8,0},{16,8},{24,16},{9,1},{17,9},{25,17},{10,2},{18,10},{26,18},{... | collective-permute-start | bytes 3145736 | tf_op jit(solution)/shard_map/ppermute | solution.py:190
  250.6 94.9 %reduce-scatter.29.cloned.1.call-start = ((), (), s32[]{:S(2)}) async-start(), calls=%async_computation.19 | async-start | bytes 1179648 | tf_op jit(solution)/shard_map/reduce_scatter | solution.py:871
  251.3 120.7 %reduce-scatter.17.cloned.1.call-start = ((), (), s32[]{:S(2)}) async-start(), calls=%async_computation.13 | async-start | bytes 589824 | tf_op jit(solution)/shard_map/reduce_scatter | solution.py:871
  337.7 76.0 %reduce-scatter.15.cloned.1.call-start = ((), (), s32[]{:S(2)}) async-start(), calls=%async_computation.12 | async-start | bytes 1769472 | tf_op jit(solution)/shard_map/reduce_scatter | solution.py:871
  338.3 119.8 %reduce-scatter.23.cloned.1.call-start = ((), (), s32[]{:S(2)}) async-start(), calls=%async_computation.16 | async-start | bytes 2359296 | tf_op jit(solution)/shard_map/reduce_scatter | solution.py:871
  338.9 163.9 %reduce-scatter.27.cloned.1.call-start = ((), (), s32[]{:S(2)}) async-start(), calls=%async_computation.18 | async-start | bytes 2359296 | tf_op jit(solution)/shard_map/reduce_scatter | solution.py:871
  339.5 205.2 %reduce-scatter.13.cloned.1.call-start = ((), (), s32[]{:S(2)}) async-start(), calls=%async_computation.11 | async-start | bytes 1769472 | tf_op jit(solution)/shard_map/reduce_scatter | solution.py:871
  340.2 249.5 %reduce-scatter.21.cloned.1.call-start = ((), (), s32[]{:S(2)}) async-start(), calls=%async_computation.15 | async-start | bytes 2359296 | tf_op jit(solution)/shard_map/reduce_scatter | solution.py:871
  340.3 2.9 copy-start.38
  340.3 4.0 copy-start.34
  341.0 293.7 %reduce-scatter.25.cloned.1.call-start = ((), (), s32[]{:S(2)}) async-start(), calls=%async_computation.17 | async-start | bytes 2359296 | tf_op jit(solution)/shard_map/reduce_scatter | solution.py:871
  341.0 293.7 %copy-start.35 = (f32[11,64]{1,0:T(8,128)S(1)}, f32[11,64]{1,0:T(8,128)}, u32[]{:S(2)}) copy-start(f32[11,64]{1,0:T(8,128)} %param.40) | copy-start | bytes 8452
  341.0 295.0 %copy-start.39 = (f32[11,64]{1,0:T(8,128)S(1)}, f32[11,64]{1,0:T(8,128)}, u32[]{:S(2)}) copy-start(f32[11,64]{1,0:T(8,128)} %param.48) | copy-start | bytes 8452
  341.0 295.7 %copy-start.40 = (f32[11,64]{1,0:T(8,128)S(1)}, f32[11,64]{1,0:T(8,128)}, u32[]{:S(2)}) copy-start(f32[11,64]{1,0:T(8,128)} %param.56) | copy-start | bytes 8452
  341.0 296.4 %copy-start.42 = (f32[8,128]{1,0:T(8,128)S(1)}, f32[8,128]{1,0:T(8,128)}, u32[]{:S(2)}) copy-start(f32[8,128]{1,0:T(8,128)} %get-tuple-element.147) | copy-start | bytes 12292
  341.1 296.5 %copy-start.15 = (bf16[1024,512]{1,0:T(8,128)(2,1)S(1)}, bf16[1024,512]{1,0:T(8,128)(2,1)}, u32[]{:S(2)}) copy-start(bf16[1024,512]{1,0:T(8,128)(2,1)} %get-tuple-element.97) | copy-start | bytes 3145732
  341.1 296.5 %copy-start.16 = (bf16[1024,512]{1,0:T(8,128)(2,1)S(1)}, bf16[1024,512]{1,0:T(8,128)(2,1)}, u32[]{:S(2)}) copy-start(bf16[1024,512]{1,0:T(8,128)(2,1)} %get-tuple-element.98) | copy-start | bytes 3145732
  341.7 337.1 %reduce-scatter.11.cloned.1.call-start = ((), (), s32[]{:S(2)}) async-start(), calls=%async_computation.10 | async-start | bytes 147456 | tf_op jit(solution)/shard_map/reduce_scatter | solution.py:871
  345.1 407.0 %all-reduce.9.cloned.1.call-start = ((), (), s32[]{:S(2)}) async-start(), calls=%async_computation.20 | async-start | bytes 3407872 | tf_op jit(solution)/shard_map/psum | solution.py:877
  637.6 138.5 %copy-start.26 = (f32[80,64]{0,1:T(8,128)S(1)}, f32[80,64]{0,1:T(8,128)}, u32[]{:S(2)}) copy-start(f32[80,64]{0,1:T(8,128)} %param.34) | copy-start | bytes 61444
  637.6 138.5 %copy-start.36 = (f32[80,64]{0,1:T(8,128)S(1)}, f32[80,64]{0,1:T(8,128)}, u32[]{:S(2)}) copy-start(f32[80,64]{0,1:T(8,128)} %param.42) | copy-start | bytes 61444
  637.6 138.5 %copy-start.37 = (f32[80,64]{0,1:T(8,128)S(1)}, f32[80,64]{0,1:T(8,128)}, u32[]{:S(2)}) copy-start(f32[80,64]{0,1:T(8,128)} %param.50) | copy-start | bytes 61444
  639.1 138.2 %copy-start.6 = (f32[2,64,1536]{2,1,0:T(8,128)S(1)}, f32[2,64,1536]{2,1,0:T(8,128)}, u32[]{:S(2)}) copy-start(f32[2,64,1536]{2,1,0:T(8,128)} %refs_6_.1) | copy-start | bytes 2359300
  639.1 138.2 %copy-start.24 = (f32[2,64,1536]{2,1,0:T(8,128)S(1)}, f32[2,64,1536]{2,1,0:T(8,128)}, u32[]{:S(2)}) copy-start(f32[2,64,1536]{2,1,0:T(8,128)} %param.43) | copy-start | bytes 2359300
  678.8 101.8 %copy-start.45 = (f32[2,8]{1,0:T(2,128)}, f32[2,8]{1,0:T(2,128)S(1)}, u32[]{:S(2)}) copy-start(f32[2,8]{1,0:T(2,128)S(1)} %get-tuple-element.273) | copy-start | bytes 196
  777.3 3.4 copy-start.17
  777.3 3.4 copy-start.27
  777.3 3.4 copy-start.28
  777.3 3.4 copy-start.29
  777.3 5.9 copy-start
  777.3 5.9 copy-start.7
  777.3 5.9 copy-start.8
  777.4 5.9 copy-start.13
  777.4 5.8 copy-start.14
  783.2 2.5 copy-start.1
  785.7 37.6 %copy-start.2 = (f32[2,64,2048]{2,1,0:T(8,128)}, f32[2,64,2048]{2,1,0:T(8,128)S(1)}, u32[]{:S(2)}) copy-start(f32[2,64,2048]{2,1,0:T(8,128)S(1)} %get-tuple-element.296) | copy-start | bytes 3145732
  785.8 2.8 copy-start.18
  785.8 2.8 copy-start.25
  785.8 2.8 copy-start.30
  785.8 2.8 copy-start.31
  785.8 4.5 copy-start.32
  785.8 4.5 copy-start.33
  816.7 5.8 copy-start.20
  816.7 5.8 copy-start.21
  819.5 3.9 copy-start.3
  (12 other events, 22.1 us)
Sparse Core Ops, SparseCore 0:
  250.7 37.5 reduce-scatter.18
  292.4 36.0 reduce-scatter.28
  337.8 34.1 reduce-scatter.16
  375.2 38.4 reduce-scatter.14
  416.8 41.1 reduce-scatter.22
  461.5 41.2 reduce-scatter.26
  506.1 38.4 reduce-scatter.12
  548.5 41.1 reduce-scatter.20
  593.4 41.2 reduce-scatter.24
  638.1 33.3 reduce-scatter.10
  675.0 77.0 all-reduce.8
